TPU v7x, 128 devices: a whole 4x4x4 slice. The times are simulated.
128 devices in a mesh: dp: 4 (over y), item: 32 (over z, x, core).
Axes of the slice: x: 4, y: 4, z: 4, core: 2. Of those that a mesh axis runs over, the one named last changes fastest.
Arguments:
- queries: bfloat16 [131072, 256], P(('dp', 'item')), may hold values from -0.5 to 0.5
- item_table: float32 [131072, 256], P('item'), may hold values from -0.5 to 0.5
- adagrad_state: float32 [131072], P('item'), may hold values from 1 to 1000
- pos_owner: int32 [131072, 1], P(('dp', 'item')), may hold values from 0 to 31; in each aligned block of 1024 rows (0 to 1023, 1024 to 2047, ...) at most 96 rows name the same one
- pos_row: int32 [131072], P(('dp', 'item')), may hold values from 0 to 4095
- neg_rows: int32 [6144], P(('dp', 'item')), may hold values from 0 to 4095
Outputs:
- query_grad: bfloat16 [131072, 256], P(('dp', 'item'))
- example_loss: float32 [131072], P(('dp', 'item'))
- new_table: float32 [131072, 256], P('item')
- new_state: float32 [131072], P('item')
Inputs may be any that keep to these rules, and one draw needn't show every extreme that they name: `pos_owner`: within the rows of one device (aligned blocks of 1024 examples) no shard is named more than 96 times; some device's block names one shard exactly 96 times.
All inputs are finite; a program needn't handle non-finite values.
Results may differ from a plain program's by a relative error of at most 0.0049.
Values may be sent and summed in bfloat16 or wider, within the bound.
A program may use at most 64 MiB of HBM per device.

v0:
```python
import math

import jax
import jax.numpy as jnp
from jax import lax
from jax.sharding import PartitionSpec as P

INV_TEMP = 20.0
LEARN_RATE = 0.05
EPSILON = 1e-06


def unit_rows(matrix):
    row_norm = jnp.sqrt(jnp.sum(matrix * matrix, axis=-1, keepdims=True) + EPSILON)
    return (matrix / row_norm, row_norm)


def on_device(queries, item_table, adagrad_state, pos_owner, pos_row, neg_rows):
    ex_count = queries.shape[0]
    rows_dev = item_table.shape[0]
    feat_width = item_table.shape[1]
    item_count = lax.axis_size("item")
    capacity = 3 * ex_count // item_count
    item_index = lax.axis_index("item")
    query_hat, query_norm = unit_rows(queries.astype(jnp.float32))
    query_send = query_hat.astype(jnp.bfloat16)
    unit_table, table_norm = unit_rows(item_table)
    table_send = unit_table.astype(jnp.bfloat16)
    owners = pos_owner[:, 0]
    onehot = (owners[:, None] == jnp.arange(item_count, dtype=jnp.int32)[None, :]).astype(jnp.int32)
    earlier = jnp.cumsum(onehot, axis=0) - onehot
    slots = jnp.sum(earlier * onehot, axis=1)
    places = owners * capacity + slots
    requests = jnp.zeros((item_count * capacity,), jnp.int32).at[places].set(pos_row)
    requests = requests.reshape(item_count, capacity)
    asked_rows = lax.all_to_all(requests, "item", split_axis=0, concat_axis=0, tiled=True)
    found = table_send[asked_rows]
    returned = lax.all_to_all(found, "item", split_axis=0, concat_axis=0, tiled=True)
    pos_e = returned.reshape(item_count * capacity, feat_width)[places]
    pos_gid = owners * rows_dev + pos_row
    my_gid = item_index * rows_dev + neg_rows
    my_neg = table_send[neg_rows]
    block_rows, block_ids = (
        lax.all_gather(my_neg, "item", axis=0, tiled=True),
        lax.all_gather(my_gid, "item", axis=0, tiled=True),
    )
    all_rows, all_ids = (
        lax.all_gather(block_rows, "dp", axis=0, tiled=True),
        lax.all_gather(block_ids, "dp", axis=0, tiled=True),
    )
    negs = all_rows.shape[0]
    block_size = math.gcd(negs, 1024)
    block_count = negs // block_size
    row_blocks = all_rows.reshape(block_count, block_size, feat_width)
    id_blocks = all_ids.reshape(block_count, block_size)

    def block_scores(row_block, id_block):
        scores = (
            jnp.einsum("ed,nd->en", query_send, row_block, preferred_element_type=jnp.float32)
            * INV_TEMP
        )
        allowed = id_block[None, :] != pos_gid[:, None]
        return (scores, allowed)

    s_pos = INV_TEMP * jnp.sum(query_send.astype(jnp.float32) * pos_e.astype(jnp.float32), axis=1)

    def add_exp(carry, pieces):
        scores, allowed = block_scores(pieces[0], pieces[1])
        return (carry + jnp.sum(jnp.where(allowed, jnp.exp(scores), 0.0), axis=1), None)

    neg_totals, _ = lax.scan(add_exp, jnp.zeros((ex_count,), jnp.float32), (row_blocks, id_blocks))
    lse = jnp.log(jnp.exp(s_pos) + neg_totals)
    example_loss = lse - s_pos

    def both_products(carry, pieces):
        scores, allowed = block_scores(pieces[0], pieces[1])
        probs = jnp.where(allowed, jnp.exp(scores - lse[:, None]), 0.0).astype(jnp.bfloat16)
        carry = carry + jnp.dot(probs, pieces[0], preferred_element_type=jnp.float32)
        partial_rows = INV_TEMP * jnp.einsum(
            "en,ed->nd", probs, query_send, preferred_element_type=jnp.float32
        )
        return (carry, partial_rows)

    neg_part, partial_blocks = lax.scan(
        both_products, jnp.zeros((ex_count, feat_width), jnp.float32), (row_blocks, id_blocks)
    )
    neg_partials = partial_blocks.reshape(negs, feat_width)
    p_pos = jnp.exp(s_pos - lse)
    g_query = INV_TEMP * ((p_pos - 1.0)[:, None] * pos_e.astype(jnp.float32) + neg_part)
    query_grad = (
        (g_query - query_hat * jnp.sum(query_hat * g_query, axis=1, keepdims=True)) / query_norm
    ).astype(jnp.bfloat16)
    g_pos = INV_TEMP * (p_pos - 1.0)[:, None] * query_hat
    outbox = jnp.zeros((item_count * capacity, feat_width), jnp.float32).at[places].set(g_pos)
    outbox = outbox.reshape(item_count, capacity, feat_width)
    inbox = lax.all_to_all(
        outbox.astype(jnp.bfloat16), "item", split_axis=0, concat_axis=0, tiled=True
    ).astype(outbox.dtype)
    dense = jnp.zeros((rows_dev, feat_width), jnp.float32)
    dense = dense.at[asked_rows.reshape(-1)].add(inbox.reshape(-1, feat_width))
    neg_grad = lax.psum_scatter(neg_partials, ("dp", "item"), scatter_dimension=0, tiled=True)
    dense = dense.at[neg_rows].add(neg_grad)
    g_unit = lax.psum(dense.astype(jnp.bfloat16), "dp").astype(jnp.float32)
    g_row = (g_unit - unit_table * jnp.sum(unit_table * g_unit, axis=1, keepdims=True)) / table_norm
    new_state = adagrad_state + jnp.mean(g_row * g_row, axis=1)
    new_table = item_table - LEARN_RATE * g_row / jnp.sqrt(new_state)[:, None]
    return (query_grad, example_loss, new_table, new_state)


def solution(mesh):
    placed = (
        P(("dp", "item"), None),
        P("item", None),
        P("item"),
        P(("dp", "item"), None),
        P(("dp", "item")),
        P(("dp", "item")),
    )
    return jax.shard_map(
        on_device,
        mesh=mesh,
        in_specs=placed,
        out_specs=(P(("dp", "item"), None), P(("dp", "item")), P("item", None), P("item")),
        check_vma=False,
    )
```

profile of v0, /device:TPU:1, one launch (start us, length us, event | category | flops | bytes accessed | tf_op | source)
XLA Modules:
  0.0 490.1 jit_solution(17192636211847905702)
XLA Ops:
  7.2 3.0 multiply_reduce_fusion.1
  10.7 0.7 fusion.33
  11.4 0.6 dynamic-slice
  12.8 0.7 gather_fusion.2
  13.5 29.8 %all-gather = bf16[1536,256]{1,0:T(8,128)(2,1)} all-gather(bf16[48,256]{1,0:T(8,128)(2,1)S(1)} %gather_fusion.2), channel_id=2, replica_groups=mesh['dp'=4,'item'=32] {'item'}, dimensions={0}, use_global_device_ids=true | all-gather | bytes 811008 | tf_op jit(solution)/shard_map/all_gather | solution.py:44
  43.3 9.0 %reduce-window.6 = s32[32,8,128]{2,1,0:T(8,128)S(1)} reduce-window(s32[32,8,128]{2,1,0:T(8,128)S(1)} %fusion.29, s32[]{:T(128)} %constant.33.clone.1), window={size=1x1x128 pad=0_0x0_0x127_0}, to_apply=%region_2.0 | reduce-window | flops 4161536 | bytes 262148 | tf_op jit(solution)/shard_map/reduce-window
  52.8 4.3 scatter_custom_fusion
  57.2 11.8 %all_to_all.22 = s32[32,1,96]{2,1,0:T(1,128)S(1)} all-to-all(s32[32,1,96]{2,1,0:T(1,128)S(1)} %all_to_all.14), channel_id=1, replica_groups=mesh['dp'=4,'item'=32] {'item'}, dimensions={0} | all-to-all | bytes 24576 | tf_op jit(solution)/shard_map/all_to_all | solution.py:36
  69.1 13.0 %gather_fusion = bf16[3072,256]{1,0:T(8,128)(2,1)} fusion(bf16[4096,256]{1,0:T(8,128)(2,1)S(1)} %fusion.33, s32[3072]{0:T(1024)S(1)} %broadcast_clamp_fusion), kind=kCustom, calls=%fused_computation | custom fusion | bytes 3158016 | tf_op jit(solution)/shard_map/gather | solution.py:37
  82.2 4.3 all-to-all-start.1
  86.6 28.8 %all-reduce = s32[1536]{0:T(1024)S(1)} all-reduce(s32[1536]{0:T(1024)S(1)} %get-tuple-element.167), channel_id=1, replica_groups=mesh['dp'=4,'item'=32] {'item'}, use_global_device_ids=true, to_apply=%add | all-reduce | flops 1536 | bytes 12288
  115.4 9.7 %all-gather.2 = s32[4,1,1536]{2,1,0:T(1,128)S(1)} all-gather(s32[1,1,1536]{2,1,0:T(1,128)S(1)} %reshape.204), channel_id=1, replica_groups=mesh['dp'=4,'item'=32] {'dp'}, dimensions={0}, use_global_device_ids=true | all-gather | bytes 30720 | tf_op jit(solution)/shard_map/all_gather | solution.py:49
  125.5 3.9 gather_fusion.1
  129.9 12.9 %while.24 = (s32[]{:T(128)}, f32[1024]{0:T(1024)S(1)}, s32[6,1024]{1,0:T(8,128)S(1)}, s32[1024]{0:T(1024)S(1)}, bf16[6,1024,256]{2,1,0:T(8,128)(2,1)}, /*index=5*/bf16[1024,256]{1,0:T(8,128)(2,1)S(1)}, s32[]{:T(128)}, s32[]{:T(128)}) while((s32[]{:T(128)}, f32[1024]{0:T(1024)S(1)}, s32[6,1024]{1,0:T(8,128)S(1)}, ...), condition=%wide.region_9.10_spmd.clone, body=%wide.region_7.9_spmd.clone.sunk | while | flops 541066240 | bytes 1081955 | solution.py:71
  130.0 2.2 fusion.54
  132.2 2.1 fusion.54
  134.3 2.1 fusion.54
  136.4 2.1 fusion.54
  138.6 2.1 fusion.54
  140.7 2.1 fusion.54
  142.8 0.6 broadcast_multiply_fusion
  143.4 48.0 %while.25 = (s32[]{:T(128)}, f32[1024,256]{1,0:T(8,128)S(1)}, f32[6,1024,256]{2,1,0:T(8,128)}, s32[6,1024]{1,0:T(8,128)S(1)}, s32[1024]{0:T(1024)S(1)}, /*index=...) while((s32[]{:T(128)}, f32[1024,256]{1,0:T(8,128)S(1)}, ...), condition=%wide.region_11.12_spmd.clone, body=%wide.region_10.11_spmd.clone.sunk | while | flops 1616642048 | bytes 19945104 | solution.py:84
  143.4 2.1 fusion.61
  145.6 1.3 copy-done.12
  146.9 1.7 fusion.62
  148.6 2.8 convolution_add_fusion.2
  151.4 2.1 fusion.61
  153.6 1.3 copy-done.12
  154.9 1.8 fusion.62
  156.7 2.8 convolution_add_fusion.2
  159.5 2.1 fusion.61
  161.7 1.3 copy-done.12
  163.0 1.7 fusion.62
  164.7 2.8 convolution_add_fusion.2
  167.5 2.1 fusion.61
  169.6 1.3 copy-done.12
  171.0 1.7 fusion.62
  172.7 2.8 convolution_add_fusion.2
  175.5 2.1 fusion.61
  177.6 1.3 copy-done.12
  178.9 1.7 fusion.62
  180.6 2.8 convolution_add_fusion.2
  183.5 2.1 fusion.61
  185.6 1.3 copy-done.12
  186.9 1.7 fusion.62
  188.7 2.8 convolution_add_fusion.2
  191.5 7.1 %scatter_custom_fusion.1 = f32[3072,256]{1,0:T(8,128)} fusion(s32[1024]{0:T(1024)S(1)} %bitcast.102, f32[]{:T(128)} %constant.31.clone.1, f32[1024]{0:T(1024)S(1)} %get-tuple-element.160, bf16[1024,256]{1,0:T(8,128)(2,1)S(1)} %copy-done.3, f32[1024]{0:T(1024)S(1)} %add_sqrt_fusion.1), kind=kCustom, calls=%fused_computation.38 | custom fusion | flops 786432 | bytes 3678212 | tf_op jit(solution)/shard_map/scatter | solution.py:94
  198.6 3.2 convert_element_type.50
  201.8 10.0 %all-to-all-start.2 = ((bf16[32,96,256]{2,1,0:T(8,128)(2,1)}), bf16[32,96,256]{2,1,0:T(8,128)(2,1)S(1)}, u32[]{:S(2)}, u32[]{:S(2)}) async-start(bf16[32,96,256]{2,1,0:T(8,128)(2,1)} %bitcast.89), calls=%async_computation.2 | async-start | bytes 3145728 | tf_op jit(solution)/shard_map/all_to_all | solution.py:96
  211.9 0.5 broadcast.160
  212.4 0.7 reduce.4
  213.2 20.9 %all-to-all-done.2 = bf16[32,96,256]{2,1,0:T(8,128)(2,1)S(1)} async-done(((bf16[32,96,256]{2,1,0:T(8,128)(2,1)}), bf16[32,96,256]{2,1,0:T(8,128)(2,1)S(1)}, u32[]{:S(2)}, u32[]{:S(2)}) %all-to-all-start.2) | async-done | bytes 1572896 | tf_op jit(solution)/shard_map/all_to_all | solution.py:96
  234.1 22.7 %scatter_custom_fusion.2 = f32[4096,256]{1,0:T(8,128)} fusion(s32[3072]{0:T(1024)S(1)} %bitcast.103, bf16[3072,256]{1,0:T(8,128)(2,1)S(1)} %bitcast.88, f32[]{:T(128)} %constant.31.clone.1), kind=kCustom, calls=%fused_computation.34 | custom fusion | flops 1572864 | bytes 5767172 | tf_op jit(solution)/shard_map/scatter-add | solution.py:100
  256.8 147.8 %reduce-scatter.2.cloned.1.call-done = f32[48,256]{1,0:T(8,128)} async-done(((f32[6144,256]{1,0:T(8,128)}), f32[48,256]{1,0:T(8,128)}) %reduce-scatter.2.cloned.1.call-update) | async-done | bytes 49168 | tf_op jit(solution)/shard_map/reduce_scatter | solution.py:101
  404.5 5.2 %scatter_fusion = f32[4096,256]{1,0:T(8,128)} fusion(f32[4096,256]{1,0:T(8,128)} %scatter_custom_fusion.2, s32[48]{0:T(128)S(1)} %get-tuple-element.166, f32[48,256]{1,0:T(8,128)} %reduce-scatter.2.cloned.1.call-done), kind=kCustom, calls=%fused_computation.6 | custom fusion | flops 12288 | bytes 147648 | tf_op jit(solution)/shard_map/scatter-add | solution.py:102
  409.8 3.8 convert_element_type.52
  413.6 0.5 multiply_reduce_fusion.2
  414.1 1.3 divide_convert_fusion
  415.3 56.3 %all-reduce.3.cloned.1.call-done = bf16[4096,256]{1,0:T(8,128)(2,1)} async-done(((bf16[4096,256]{1,0:T(8,128)(2,1)}), bf16[4096,256]{1,0:T(8,128)(2,1)}) %all-reduce.3.cloned.1.call-update) | async-done | bytes 2097168 | tf_op jit(solution)/shard_map/psum | solution.py:103
  471.7 3.9 fusion.13
  475.7 0.7 copy-done.2
  476.4 2.0 multiply_reduce_fusion
  478.4 0.6 fusion.34
  479.0 4.5 divide_subtract_fusion
  (85 shorter events, 2.6 us)
Async XLA Ops:
  7.2 122.8 %all-gather.5.cloned.1.call-start = ((), (), s32[]{:S(2)}) async-start(), calls=%async_computation.6 | async-start | bytes 3932160 | tf_op jit(solution)/shard_map/all_gather | solution.py:48
  7.2 3.5 copy-start
  10.2 1.2 copy-start.11
  10.2 2.5 copy-start.10
  10.2 33.0 %copy-start.7 = (s32[1024,1]{0,1:T(1,128)S(1)}, s32[1024,1]{0,1:T(1,128)}, u32[]{:S(2)}) copy-start(s32[1024,1]{0,1:T(1,128)} %param.13) | copy-start | bytes 12292
  10.7 42.1 %copy-start.9 = (s32[1024]{0:T(1024)S(1)}, s32[1024]{0:T(1024)}, u32[]{:S(2)}) copy-start(s32[1024]{0:T(1024)} %param.14) | copy-start | bytes 12292
  69.1 56.1 %copy-start.3 = (bf16[1024,256]{1,0:T(8,128)(2,1)S(1)}, bf16[1024,256]{1,0:T(8,128)(2,1)}, u32[]{:S(2)}) copy-start(bf16[1024,256]{1,0:T(8,128)(2,1)} %param.10) | copy-start | bytes 1572868
  82.2 43.3 %all-to-all-start.1 = ((bf16[32,96,256]{2,1,0:T(8,128)(2,1)}), bf16[32,96,256]{2,1,0:T(8,128)(2,1)S(1)}, u32[]{:S(2)}, u32[]{:S(2)}) async-start(bf16[32,96,256]{2,1,0:T(8,128)(2,1)} %bitcast.90), calls=%async_computation.1 | async-start | bytes 3145728 | tf_op jit(solution)/shard_map/all_to_all | solution.py:38
  86.5 318.0 %reduce-scatter.2.cloned.1.call-start = ((), (), s32[]{:S(2)}) async-start(), calls=%async_computation.4 | async-start | bytes 6340608 | tf_op jit(solution)/shard_map/reduce_scatter | solution.py:101
  129.9 13.5 %copy-start.4 = (f32[1024,256]{1,0:T(8,128)S(1)}, f32[1024,256]{1,0:T(8,128)}, u32[]{:S(2)}) copy-start(f32[1024,256]{1,0:T(8,128)} %custom-call.1) | copy-start | bytes 3145732
  145.6 1.3 copy-start.12
  153.6 1.3 copy-start.12
  161.6 1.3 copy-start.12
  169.6 1.3 copy-start.12
  177.6 1.3 copy-start.12
  185.6 1.3 copy-start.12
  191.5 7.2 %copy-start.5 = (f32[1024,256]{1,0:T(8,128)}, f32[1024,256]{1,0:T(8,128)S(1)}, u32[]{:S(2)}) copy-start(f32[1024,256]{1,0:T(8,128)S(1)} %get-tuple-element.80) | copy-start | bytes 3145732
  201.8 32.3 %all-to-all-start.2 = ((bf16[32,96,256]{2,1,0:T(8,128)(2,1)}), bf16[32,96,256]{2,1,0:T(8,128)(2,1)S(1)}, u32[]{:S(2)}, u32[]{:S(2)}) async-start(bf16[32,96,256]{2,1,0:T(8,128)(2,1)} %bitcast.89), calls=%async_computation.2 | async-start | bytes 3145728 | tf_op jit(solution)/shard_map/all_to_all | solution.py:96
  211.8 259.9 %all-reduce.3.cloned.1.call-start = ((), (), s32[]{:S(2)}) async-start(), calls=%async_computation.5 | async-start | bytes 4194304 | tf_op jit(solution)/shard_map/psum | solution.py:103
  409.8 3.8 copy-start.6
  471.7 4.1 copy-start.1
  471.7 4.7 copy-start.2
  476.4 2.0 copy-start.8
Sparse Core Ops, SparseCore 0:
  43.4 38.4 all-gather.4
  191.6 212.8 reduce-scatter.1
  413.7 57.9 all-reduce.2
where the time goes:
time: 491 us; the launch traced here: 490 us
  waiting for transfers between devices  225 us (46%)
  blocking collectives  80.1 us (16%)
  other arithmetic  69.9 us (14%)
  matrix products  52.4 us (11%)
  local copies, waits for them, and re-layouts  32.9 us (7%)
  between operations  14.8 us (3%)
  starting transfers between devices  14.4 us (3%)
    reduce_scatter x1, waiting for transfers between devices, on_device(): lax.psum_scatter(neg_partials, ('dp', 'item'), scatter_dimension=0, tiled...  148 us
    psum x1, waiting for transfers between devices, on_device(): g_unit = lax.psum(dense.astype(jnp.bfloat16), 'dp').astype(jnp.float32)  56.3 us
    all_gather x1, blocking collectives, on_device(): lax.all_gather(my_neg, 'item', axis=0, tiled=True)  29.8 us
    unnamed x1, blocking collectives  28.8 us
    dot_general x12, matrix products, block_scores(): jnp.einsum('ed,nd->en', query_send, row_block, preferred_element_type=jnp...  25.4 us
    scatter-add x1, other arithmetic, on_device(): dense = dense.at[asked_rows.reshape(-1)].add(inbox.reshape(-1, feat_width))  22.7 us
    all_to_all x1, waiting for transfers between devices, on_device(): lax.all_to_all(outbox.astype(jnp.bfloat16), 'item', split_axis=0, concat_...  20.9 us
    dot_general x6, matrix products, both_products(): jnp.dot(probs, pieces[0], preferred_element_type=jnp.float32)  16.7 us
  transfers between devices with their start and end apart: 5, of which 3 were waited for; matrix products, arithmetic and copies ran while one was open for 14% of the time, Pallas kernels for 0%

commit v1 on v0

v1 whole, which is shorter than its diff:
```python
import functools

import jax
import jax.numpy as jnp
from jax import lax
from jax.experimental import pallas as pl
from jax.experimental.pallas import tpu as pltpu
from jax.sharding import PartitionSpec as P

INV_TEMP = 20.0
LEARN_RATE = 0.05
EPSILON = 1e-06
LOG2E = 1.4426950408889634
BF, F32 = jnp.bfloat16, jnp.float32
LANES = 128


def dot(a, b):
    return jnp.dot(a, b, preferred_element_type=F32)


def iota(shape, dim):
    return lax.broadcasted_iota(jnp.int32, shape, dim).astype(F32)


def eye():
    return lax.broadcasted_iota(jnp.int32, (LANES, LANES), 0) == lax.broadcasted_iota(jnp.int32, (LANES, LANES), 1)


def row_to_col(row):
    parts = []
    for k in range(row.shape[1] // LANES):
        wide = jnp.broadcast_to(row[:, k * LANES : (k + 1) * LANES], (LANES, LANES))
        parts.append(jnp.sum(jnp.where(eye(), wide, 0.0), axis=1, keepdims=True))
    return parts[0] if len(parts) == 1 else jnp.concatenate(parts, axis=0)


def col_to_row(col):
    parts = []
    for k in range(col.shape[0] // LANES):
        wide = jnp.broadcast_to(col[k * LANES : (k + 1) * LANES], (LANES, LANES))
        parts.append(jnp.sum(jnp.where(eye(), wide, 0.0), axis=0, keepdims=True))
    return parts[0] if len(parts) == 1 else jnp.concatenate(parts, axis=1)


def main_kernel(
    n_dp, n_item,
    q_ref, table_ref, owner_ref, row_ref, neg_ref,
    grad_ref, loss_ref, g_ref, negsum_ref, negid_ref,
    tsend, qt, req_out, req_in, negbuf, nidbuf, found, returned, outbox, inbox, acc, ut, tot, et, part, sib_in, red_in, red_out, y_in,
    dense_f, rs_out, relay_in, rs_in, ag,
    req_s, req_r, neg_s, neg_r, nid_s, nid_r, pos_s, pos_r, g_s, g_r, sib_s, sib_r, red_s, red_r, y_s, y_r,
    rs_s, relay_r, rs_r, ag_s, ag_r,
):
    ex, width = q_ref.shape
    rows = table_ref.shape[0]
    chips = n_item // 2
    cap = 3 * ex // n_item
    neg = negbuf.shape[2]
    y, me = lax.axis_index("dp"), lax.axis_index("item")
    chip, core = me // 2, lax.rem(me, 2)
    sibling = chip * 2 + 1 - core
    up, far, down = lax.rem(y + 1, n_dp), lax.rem(y + 2, n_dp), lax.rem(y + 3, n_dp)

    def copy(src, dst, send, recv, **where):
        return pltpu.make_async_remote_copy(
            src_ref=src, dst_ref=dst, send_sem=send, recv_sem=recv, device_id=where, device_id_type=pl.DeviceIdType.MESH
        )

    barrier = pltpu.get_barrier_semaphore()

    @pl.loop(1, n_item)
    def _(off):
        pl.semaphore_signal(barrier, inc=1, device_id={"item": lax.rem(me + off, n_item)}, device_id_type=pl.DeviceIdType.MESH)

    @pl.loop(1, n_dp)
    def _(off):
        pl.semaphore_signal(barrier, inc=1, device_id={"dp": lax.rem(y + off, n_dp)}, device_id_type=pl.DeviceIdType.MESH)

    owner_c = owner_ref[...].astype(F32)
    row_r = row_ref[...].astype(F32)
    row_c = row_to_col(row_r)
    owner_r = col_to_row(owner_c)
    gid_r = owner_r * rows + row_r
    onehot_c = (owner_c == iota((ex, LANES), 1)).astype(F32)
    before = (iota((ex, ex), 1) < iota((ex, ex), 0)).astype(BF)
    slot_c = jnp.sum(dot(before, onehot_c.astype(BF)) * onehot_c, axis=1, keepdims=True)
    place_c = owner_c * cap + slot_c
    place_r = col_to_row(place_c)
    high_c = jnp.floor(row_c * (1.0 / 64.0))
    low_c = row_c - 64.0 * high_c
    at_slot = slot_c == iota((ex, LANES), 1)
    both = jnp.concatenate([jnp.where(at_slot, high_c, 0.0), jnp.where(at_slot, low_c, 0.0)], axis=1).astype(BF)
    owners_r = (owner_r == iota((n_item, ex), 0)).astype(BF)
    asked2 = dot(owners_r, both)
    asked = asked2[:, :LANES] * 64.0 + asked2[:, LANES:]
    for s in range(n_item):
        req_out[s] = asked[s : s + 1, :]

    tile = min(512, rows)

    @pl.loop(0, rows // tile)
    def _(k):
        at = pl.ds(pl.multiple_of(k * tile, tile), tile)
        t = table_ref[at, :]
        tsend[at, :] = (t / jnp.sqrt(jnp.sum(t * t, axis=1, keepdims=True) + EPSILON)).astype(BF)

    neg_row = neg_ref[...].astype(F32)
    neg_c = row_to_col(neg_row)[:neg]
    mine = y * 2 + core
    my_neg = jnp.zeros((neg, width), F32)
    for k in range(rows // tile):
        pick = (neg_c == iota((neg, tile), 1) + float(k * tile)).astype(BF)
        my_neg += dot(pick, tsend[k * tile : (k + 1) * tile, :])
    negbuf[mine, chip] = my_neg.astype(BF)
    nidbuf[mine, chip] = neg_row

    pl.semaphore_wait(barrier, n_item - 1 + n_dp - 1)

    req_in[me] = req_out[me]

    def req_copy(peer):
        return copy(req_out.at[peer], req_in.at[me], req_s.at[peer], req_r.at[me], item=peer)

    @pl.loop(1, n_item)
    def _(off):
        req_copy(lax.rem(me + off, n_item)).start()

    def plane_copies(peer_chip):
        to = peer_chip * 2 + core
        return (
            copy(negbuf.at[mine, chip], negbuf.at[mine, chip], neg_s.at[peer_chip], neg_r.at[chip], item=to),
            copy(nidbuf.at[mine, chip], nidbuf.at[mine, chip], nid_s.at[peer_chip], nid_r.at[chip], item=to),
        )

    @pl.loop(1, chips)
    def _(off):
        for c in plane_copies(lax.rem(chip + off, chips)):
            c.start()

    q = q_ref[...].astype(F32)
    q_norm = jnp.sqrt(jnp.sum(q * q, axis=1, keepdims=True) + EPSILON)
    acc[...] = q / q_norm
    qt[...] = jnp.transpose(acc[...]).astype(BF)

    def wait_recv(dst, send, recv, **where):
        copy(dst, dst, send, recv, **where).wait_recv()

    @pl.loop(1, chips)
    def _(off):
        src = lax.rem(chip + off, chips)
        wait_recv(negbuf.at[mine, src], neg_s.at[src], neg_r.at[src], item=src * 2 + core)
        wait_recv(nidbuf.at[mine, src], nid_s.at[src], nid_r.at[src], item=src * 2 + core)

    pieces = 2 * n_dp

    def y_copies(dest):
        at = chips + mine
        s_at = chips + dest
        return (
            copy(negbuf.at[mine], negbuf.at[mine], neg_s.at[s_at], neg_r.at[at], dp=dest),
            copy(nidbuf.at[mine], nidbuf.at[mine], nid_s.at[s_at], nid_r.at[at], dp=dest),
        )

    def sib_copies(piece):
        at = chips + pieces + piece
        return (
            copy(negbuf.at[piece], negbuf.at[piece], neg_s.at[at], neg_r.at[at], item=sibling),
            copy(nidbuf.at[piece], nidbuf.at[piece], nid_s.at[at], nid_r.at[at], item=sibling),
        )

    @pl.loop(1, n_dp)
    def _(off):
        for c in y_copies(lax.rem(y + off, n_dp)):
            c.start()

    for c in sib_copies(mine):
        c.start()

    @pl.loop(1, n_item)
    def _(off):
        src = lax.rem(me + off, n_item)
        wait_recv(req_in.at[src], req_s.at[src], req_r.at[src], item=src)

    batch = min(8, n_item)
    batches = n_item // batch

    def pos_copy(peer):
        return copy(found.at[peer], returned.at[me], pos_s.at[peer], pos_r.at[me], item=peer)

    @pl.loop(0, batches)
    def _(k):
        first = lax.rem(k + me // batch, batches) * batch
        ids = jnp.concatenate([row_to_col(req_in[first + s])[:cap] for s in range(batch)], axis=0)
        got = jnp.zeros((batch * cap, width), F32)
        for t in range(rows // tile):
            pick = (ids == iota((batch * cap, tile), 1) + float(t * tile)).astype(BF)
            got += dot(pick, tsend[t * tile : (t + 1) * tile, :])
        found[pl.ds(first, batch)] = got.astype(BF).reshape(batch, cap, width)
        for s in range(batch):

            @pl.when(first + s != me)
            def _():
                pos_copy(first + s).start()

    returned[me] = found[me]

    tot[...] = jnp.zeros_like(tot)
    ut[...] = jnp.zeros_like(ut)
    half = max(1, chips // 2)

    def pass1(piece):
        @pl.loop(0, chips // half)
        def _(h):
            first = h * half
            block = negbuf[piece, pl.ds(first, half)].reshape(half * neg, width)
            ids = jnp.concatenate(
                [
                    row_to_col(nidbuf[piece, first + z])[:neg]
                    + (((first + z) * 2 + lax.rem(piece, 2)) * rows).astype(F32)
                    for z in range(half)
                ],
                axis=0,
            )
            e = jnp.where(ids != gid_r, jnp.exp2(dot(block, qt[...]) * (INV_TEMP * LOG2E)), 0.0)
            tot[...] += jnp.sum(e.reshape(half * neg // 8, 8, ex), axis=0)
            eb = e.astype(BF)
            et[piece, pl.ds(first, half)] = eb.reshape(half, neg, ex)
            ut[...] += lax.dot_general(block, eb, (((0,), (0,)), ((), ())), preferred_element_type=F32)

    pass1(mine)

    @pl.loop(0, n_dp)
    def _(off):
        @pl.when(off > 0)
        def _():
            piece = lax.rem(y + off, n_dp) * 2 + core
            wait_recv(negbuf.at[piece], neg_s.at[chips + piece // 2], neg_r.at[chips + piece], dp=piece // 2)
            wait_recv(nidbuf.at[piece], nid_s.at[chips + piece // 2], nid_r.at[chips + piece], dp=piece // 2)
            for c in sib_copies(piece):
                c.start()
            pass1(piece)

    @pl.loop(0, n_dp)
    def _(off):
        piece = lax.rem(y + off, n_dp) * 2 + 1 - core
        at = chips + pieces + piece
        wait_recv(negbuf.at[piece], neg_s.at[at], neg_r.at[at], item=sibling)
        wait_recv(nidbuf.at[piece], nid_s.at[at], nid_r.at[at], item=sibling)
        pass1(piece)

    @pl.loop(1, n_item)
    def _(off):
        src = lax.rem(me + off, n_item)
        wait_recv(returned.at[src], pos_s.at[src], pos_r.at[src], item=src)

    q_hat = acc[...]
    pos_e = jnp.zeros((ex, width), F32)
    for k in range(batches):
        pick = (place_c == iota((ex, batch * cap), 1) + float(k * batch * cap)).astype(BF)
        pos_e += dot(pick, returned[k * batch : (k + 1) * batch].reshape(batch * cap, width))
    s_pos = INV_TEMP * jnp.sum(q_hat.astype(BF).astype(F32) * pos_e, axis=1, keepdims=True)
    neg_tot = row_to_col(jnp.sum(tot[...], axis=0, keepdims=True))
    lse = jnp.log(jnp.exp(s_pos) + neg_tot)
    loss_ref[...] = col_to_row(lse - s_pos)
    coef = jnp.exp(s_pos - lse) - 1.0
    inv_tot = jnp.exp(-lse)

    g_pos = (INV_TEMP * coef * q_hat).astype(BF)

    def g_copy(peer):
        return copy(outbox.at[peer], inbox.at[me], g_s.at[peer], g_r.at[me], item=peer)

    for k in range(batches):
        pick = (place_r == iota((batch * cap, ex), 0) + float(k * batch * cap)).astype(BF)
        outbox[k * batch : (k + 1) * batch] = dot(pick, g_pos).astype(BF).reshape(batch, cap, width)

    @pl.loop(1, n_item)
    def _(off):
        g_copy(lax.rem(me + off, n_item)).start()

    inbox[me] = outbox[me]

    q_scaled = (q_hat.astype(BF).astype(F32) * (INV_TEMP * inv_tot)).astype(BF)

    def pass2(side):
        @pl.loop(0, n_dp)
        def _(d):
            for h in range(chips // half):
                at = slice(h * half, (h + 1) * half)
                p = dot(et[d * 2 + side, at].reshape(half * neg, ex), q_scaled)
                p = p.astype(BF).reshape(half, neg, width)
                for z in range(half):
                    part[side, h * half + z, pl.ds(pl.multiple_of(d * neg, neg), neg), :] = p[z]

    pass2(1 - core)
    to_sib = copy(part.at[1 - core], sib_in, sib_s, sib_r, item=sibling)
    to_sib.start()
    pass2(core)

    g_q = INV_TEMP * (coef * pos_e + jnp.transpose(ut[...]) * inv_tot)
    grad_ref[...] = ((g_q - q_hat * jnp.sum(q_hat * g_q, axis=1, keepdims=True)) / q_norm).astype(BF)

    to_sib.wait_recv()

    @pl.loop(0, chips)
    def _(z):
        red_out[z] = (part[core, z].astype(F32) + sib_in[z].astype(F32)).astype(BF)

    @pl.loop(1, n_item)
    def _(off):
        src = lax.rem(me + off, n_item)
        wait_recv(inbox.at[src], g_s.at[src], g_r.at[src], item=src)

    def red_copy(peer_chip):
        return copy(red_out.at[peer_chip], red_in.at[chip], red_s.at[peer_chip], red_r.at[chip], item=peer_chip * 2 + core)

    @pl.loop(1, chips)
    def _(off):
        red_copy(lax.rem(chip + off, chips)).start()

    quarter = rows // n_dp
    hq = quarter // 2
    four = 4

    def dense(dest):
        dense_f[...] = jnp.zeros_like(dense_f)

        @pl.loop(0, n_item // four)
        def _(k):
            ids = jnp.concatenate([req_in[k * four + s][:, :cap] for s in range(four)], axis=1)
            base = (dest * quarter).astype(F32)
            pick = (ids == iota((quarter, four * cap), 0) + base).astype(BF)
            dense_f[...] += dot(pick, inbox[pl.ds(k * four, four)].reshape(four * cap, width))

    def rs_copies():
        return (
            copy(rs_out.at[0, 0], relay_in.at[0], rs_s.at[0, 0], relay_r.at[0], dp=up),
            copy(rs_out.at[0, 1], relay_in.at[1], rs_s.at[0, 1], relay_r.at[1], dp=down),
            copy(rs_out.at[1, 0], rs_in.at[0, 0], rs_s.at[1, 0], rs_r.at[0, 0], dp=up),
            copy(rs_out.at[1, 1], rs_in.at[0, 1], rs_s.at[1, 1], rs_r.at[0, 1], dp=up),
            copy(rs_out.at[2, 0], rs_in.at[1, 0], rs_s.at[2, 0], rs_r.at[1, 0], dp=down),
            copy(rs_out.at[2, 1], rs_in.at[1, 1], rs_s.at[2, 1], rs_r.at[1, 1], dp=down),
        )

    far0, far1, up0, up1, down0, down1 = rs_copies()
    dense(far)
    rs_out[0, 0] = dense_f[:hq, :].astype(BF)
    rs_out[0, 1] = dense_f[hq:, :].astype(BF)
    far0.start()
    far1.start()
    dense(up)
    rs_out[1, 1] = dense_f[hq:, :].astype(BF)
    up1.start()
    far0.wait_recv()
    rs_out[1, 0] = (dense_f[:hq, :] + relay_in[0].astype(F32)).astype(BF)
    up0.start()
    dense(down)
    rs_out[2, 0] = dense_f[:hq, :].astype(BF)
    down0.start()
    far1.wait_recv()
    rs_out[2, 1] = (dense_f[hq:, :] + relay_in[1].astype(F32)).astype(BF)
    down1.start()
    dense(y)

    total = red_out[chip].astype(F32)

    def add_red(off, total):
        src = lax.rem(chip + off, chips)
        wait_recv(red_in.at[src], red_s.at[src], red_r.at[src], item=src * 2 + core)
        return total + red_in[src].astype(F32)

    total = lax.fori_loop(1, chips, add_red, total)
    y_in[y] = total.astype(BF)

    def sum_copy(dest):
        return copy(y_in.at[y], y_in.at[y], y_s.at[dest], y_r.at[y], dp=dest)

    @pl.loop(1, n_dp)
    def _(off):
        sum_copy(lax.rem(y + off, n_dp)).start()

    up1.wait_recv()
    up0.wait_recv()
    down0.wait_recv()
    down1.wait_recv()
    for h in range(2):
        at = slice(h * hq, (h + 1) * hq)
        ag[y, h] = (dense_f[at, :] + rs_in[0, h].astype(F32) + rs_in[1, h].astype(F32)).astype(BF)

    def ag_copy(slot, h, way, dest):
        return copy(ag.at[slot, h], ag.at[slot, h], ag_s.at[way, h], ag_r.at[slot, h], dp=dest)

    for h in range(2):
        ag_copy(y, h, 0, up).start()
        ag_copy(y, h, 1, down).start()
    wait_recv(ag.at[down, 0], ag_s.at[0, 0], ag_r.at[down, 0], dp=down)
    ag_copy(down, 0, 2, up).start()
    wait_recv(ag.at[up, 1], ag_s.at[0, 1], ag_r.at[up, 1], dp=up)
    ag_copy(up, 1, 2, down).start()

    @pl.loop(1, n_dp)
    def _(off):
        src = lax.rem(y + off, n_dp)
        wait_recv(y_in.at[src], y_s.at[src], y_r.at[src], dp=src)

    sums = y_in[0].astype(F32)
    for d in range(1, n_dp):
        sums += y_in[d].astype(F32)
    negsum_ref[...] = sums
    for d in range(n_dp):
        negid_ref[d : d + 1, :] = nidbuf[d * 2 + core, chip]

    wait_recv(ag.at[down, 1], ag_s.at[0, 1], ag_r.at[down, 1], dp=down)
    wait_recv(ag.at[up, 0], ag_s.at[0, 0], ag_r.at[up, 0], dp=up)
    wait_recv(ag.at[far, 0], ag_s.at[0, 0], ag_r.at[far, 0], dp=down)
    wait_recv(ag.at[far, 1], ag_s.at[0, 1], ag_r.at[far, 1], dp=up)
    g_ref[...] = ag[...].reshape(rows, width)

    @pl.loop(1, n_item)
    def _(off):
        peer = lax.rem(me + off, n_item)
        req_copy(peer).wait_send()
        pos_copy(peer).wait_send()
        g_copy(peer).wait_send()

    @pl.loop(1, chips)
    def _(off):
        peer = lax.rem(chip + off, chips)
        for c in plane_copies(peer):
            c.wait_send()
        red_copy(peer).wait_send()

    @pl.loop(1, n_dp)
    def _(off):
        dest = lax.rem(y + off, n_dp)
        for c in y_copies(dest):
            c.wait_send()
        sum_copy(dest).wait_send()

    @pl.loop(0, n_dp)
    def _(d):
        for c in sib_copies(d * 2 + core):
            c.wait_send()

    to_sib.wait_send()
    for c in rs_copies():
        c.wait_send()
    for h in range(2):
        ag_copy(y, h, 0, up).wait_send()
        ag_copy(y, h, 1, down).wait_send()
    ag_copy(down, 0, 2, up).wait_send()
    ag_copy(up, 1, 2, down).wait_send()


def step_kernel(g_ref, negsum_ref, negid_ref, table_ref, state_ref, table_out, state_out):
    tile, width = g_ref.shape
    neg = negsum_ref.shape[0] // negid_ref.shape[0]
    base = (pl.program_id(0) * tile).astype(F32)
    g = g_ref[...].astype(F32)
    numbers = iota((tile, LANES), 0) + base
    ids = jnp.concatenate([negid_ref[d : d + 1, :][:, :neg] for d in range(negid_ref.shape[0])], axis=1)
    sums = negsum_ref[...]
    high = sums.astype(BF)
    pick = (ids == iota((tile, negsum_ref.shape[0]), 0) + base).astype(BF)
    g += dot(pick, high) + dot(pick, (sums - high.astype(F32)).astype(BF))
    t = table_ref[...]
    norm = jnp.sqrt(jnp.sum(t * t, axis=1, keepdims=True) + EPSILON)
    unit = t / norm
    g_row = (g - unit * jnp.sum(unit * g, axis=1, keepdims=True)) / norm
    mean = jnp.sum(g_row * g_row, axis=1, keepdims=True) * (1.0 / width)
    state_r = state_ref[...] + col_to_row(mean)
    state_out[...] = state_r
    table_out[...] = t - LEARN_RATE * g_row / jnp.sqrt(row_to_col(state_r))
    del numbers


def on_device(n_dp, n_item, queries, item_table, adagrad_state, pos_owner, pos_row, neg_rows):
    ex, width = queries.shape
    rows = item_table.shape[0]
    neg = neg_rows.shape[0]
    chips = n_item // 2
    cap = 3 * ex // n_item
    quarter = rows // n_dp
    vmem = pl.BlockSpec(memory_space=pltpu.VMEM)
    dma = pltpu.SemaphoreType.DMA
    negr = jnp.pad(neg_rows, (0, LANES - neg), constant_values=-1).reshape(1, LANES)
    n_neg = 2 * n_dp * chips * neg
    flops = 2 * width * (3 * n_neg * ex + 3 * n_item * cap * (rows + ex))
    grad, loss, g, negsum, negid = pl.pallas_call(
        functools.partial(main_kernel, n_dp, n_item),
        out_shape=(
            jax.ShapeDtypeStruct((ex, width), BF),
            jax.ShapeDtypeStruct((1, ex), F32),
            jax.ShapeDtypeStruct((rows, width), BF),
            jax.ShapeDtypeStruct((n_dp * neg, width), F32),
            jax.ShapeDtypeStruct((n_dp, LANES), F32),
        ),
        in_specs=[vmem] * 5,
        out_specs=(vmem,) * 5,
        scratch_shapes=[
            pltpu.VMEM((rows, width), BF),
            pltpu.VMEM((width, ex), BF),
            pltpu.VMEM((n_item, 1, LANES), F32),
            pltpu.VMEM((n_item, 1, LANES), F32),
            pltpu.VMEM((2 * n_dp, chips, neg, width), BF),
            pltpu.VMEM((2 * n_dp, chips, 1, LANES), F32),
            pltpu.VMEM((n_item, cap, width), BF),
            pltpu.VMEM((n_item, cap, width), BF),
            pltpu.VMEM((n_item, cap, width), BF),
            pltpu.VMEM((n_item, cap, width), BF),
            pltpu.VMEM((ex, width), F32),
            pltpu.VMEM((width, ex), F32),
            pltpu.VMEM((8, ex), F32),
            pltpu.VMEM((2 * n_dp, chips, neg, ex), BF),
            pltpu.VMEM((2, chips, n_dp * neg, width), BF),
            pltpu.VMEM((chips, n_dp * neg, width), BF),
            pltpu.VMEM((chips, n_dp * neg, width), BF),
            pltpu.VMEM((chips, n_dp * neg, width), BF),
            pltpu.VMEM((n_dp, n_dp * neg, width), BF),
            pltpu.VMEM((quarter, width), F32),
            pltpu.VMEM((3, 2, quarter // 2, width), BF),
            pltpu.VMEM((2, quarter // 2, width), BF),
            pltpu.VMEM((2, 2, quarter // 2, width), BF),
            pltpu.VMEM((n_dp, 2, quarter // 2, width), BF),
            dma((n_item,)), dma((n_item,)),
            dma((chips + 4 * n_dp,)), dma((chips + 4 * n_dp,)),
            dma((chips + 4 * n_dp,)), dma((chips + 4 * n_dp,)),
            dma((n_item,)), dma((n_item,)),
            dma((n_item,)), dma((n_item,)),
            dma, dma,
            dma((chips,)), dma((chips,)),
            dma((n_dp,)), dma((n_dp,)),
            dma((3, 2)), dma((2,)), dma((2, 2)),
            dma((3, 2)), dma((n_dp, 2)),
        ],
        compiler_params=pltpu.CompilerParams(collective_id=0, has_side_effects=True, vmem_limit_bytes=62 * 2**20),
        cost_estimate=pl.CostEstimate(flops=flops, bytes_accessed=12 * 2**20, transcendentals=n_neg * ex),
        name="loss_and_gradients",
    )(queries, item_table, pos_owner, pos_row.reshape(1, ex), negr)

    tile = min(512, rows)
    new_table, new_state = pl.pallas_call(
        step_kernel,
        grid=(rows // tile,),
        out_shape=(
            jax.ShapeDtypeStruct((rows, width), F32),
            jax.ShapeDtypeStruct((1, rows), F32),
        ),
        in_specs=[
            pl.BlockSpec((tile, width), lambda i: (i, 0)),
            pl.BlockSpec((n_dp * neg, width), lambda i: (0, 0)),
            pl.BlockSpec((n_dp, LANES), lambda i: (0, 0)),
            pl.BlockSpec((tile, width), lambda i: (i, 0)),
            pl.BlockSpec((1, tile), lambda i: (0, i)),
        ],
        out_specs=(
            pl.BlockSpec((tile, width), lambda i: (i, 0)),
            pl.BlockSpec((1, tile), lambda i: (0, i)),
        ),
        name="adagrad_step",
    )(g, negsum, negid, item_table, adagrad_state.reshape(1, rows))
    return grad, loss.reshape(ex), new_table, new_state.reshape(rows)


def solution(mesh):
    both = ("dp", "item")
    return jax.shard_map(
        functools.partial(on_device, mesh.shape["dp"], mesh.shape["item"]),
        mesh=mesh,
        in_specs=(P(both, None), P("item", None), P("item"), P(both, None), P(both), P(both)),
        out_specs=(P(both, None), P(both), P("item", None), P("item")),
        check_vma=False,
    )
```

time: 491 us -> 150 us (0.31)
  waiting for transfers between devices: 225 us -> 0 us
  Pallas kernels: 0 us -> 144 us
  blocking collectives: 80.1 us -> 0 us
  other arithmetic: 69.9 us -> 0 us
  matrix products: 52.4 us -> 0 us
  local copies, waits for them, and re-layouts: 32.9 us -> 4.27 us
  starting transfers between devices: 14.4 us -> 0 us
  between operations: 14.8 us -> 0.66 us
    reduce_scatter x1 -> x0, waiting for transfers between devices: 148 us -> none  [on_device(): lax.psum_scatter(neg_partials, ('dp', 'item'), scatter_dimension=0, tiled...]
    pallas_call x0 -> x2, Pallas kernels: none -> 144 us  [the longest x1 134 us: on_device(): pl.pallas_call(functools.partial(main_kernel, n_dp, n_item), out_shape=(j...]
    psum x1 -> x0, waiting for transfers between devices: 56.3 us -> none  [on_device(): g_unit = lax.psum(dense.astype(jnp.bfloat16), 'dp').astype(jnp.float32)]
    dot_general x24 -> x0, matrix products: 52.4 us -> none  [the longest x12 25.4 us: block_scores(): jnp.einsum('ed,nd->en', query_send, row_block, preferred_element_type=jnp...]
    all_gather x2 -> x0, blocking collectives: 39.5 us -> none  [the longest x1 29.8 us: on_device(): lax.all_gather(my_neg, 'item', axis=0, tiled=True)]
    unnamed x1 -> x0, blocking collectives: 28.8 us -> none
    scatter-add x2 -> x0, other arithmetic: 27.9 us -> none  [the longest x1 22.7 us: on_device(): dense = dense.at[asked_rows.reshape(-1)].add(inbox.reshape(-1, feat_width))]
    all_to_all x2 -> x0, waiting for transfers between devices: 20.9 us -> none  [the longest x1 20.9 us: on_device(): lax.all_to_all(outbox.astype(jnp.bfloat16), 'item', split_axis=0, concat_...]
  transfers between devices with their start and end apart: 5 -> 0, of which waited for: 3 -> 0; matrix products, arithmetic and copies ran while one was open for 14% -> 0% of each run, Pallas kernels for 0% -> 0%
where the time goes in v1:
time: 150 us; the launch traced here: 149 us
  Pallas kernels  144 us (96%)
  local copies, waits for them, and re-layouts  4.27 us (3%)
    pallas_call x1, Pallas kernels, on_device(): pl.pallas_call(functools.partial(main_kernel, n_dp, n_item), out_shape=(j...  134 us
    pallas_call x1, Pallas kernels, on_device(): pl.pallas_call(step_kernel, grid=(rows // tile,), out_shape=(jax.ShapeDty...  10.5 us
    unnamed x7, local copies, waits for them, and re-layouts  3.1 us

profile of v1, /device:TPU:1, one launch (start us, length us, event | category | flops | bytes accessed | tf_op | source)
XLA Modules:
  0.0 148.9 jit_solution(4382136326450797213)
XLA Ops:
  0.6 1.2 pad_bitcast_fusion.neg_ref
  1.8 1.7 %copy.10.owner_ref = s32[1024,1]{1,0:T(8,128)} copy(s32[1024,1]{0,1:T(1,128)} %param.9) | data formatting | bytes 8192 | tf_op args[3]
  3.5 133.5 %loss_and_gradients.1 = (bf16[1024,256]{1,0:T(8,128)(2,1)}, f32[1,1024]{1,0:T(1,128)}, bf16[4096,256]{1,0:T(8,128)(2,1)}, f32[192,256]{1,0:T(8,128)}, f32[4,128]{1,0:T(4,128)}) custom-call(bf16[1024,256]{1,0:T(8,128)(2,1)} %q_ref.1, f32[4096,256]{1,0:T(8,128)} %table_ref.3, s32[1024,1]{1,0:T(8,128)} %copy.10.owner_ref, s32[1,1024]{1,0:T(1,128)} %bitcast.9, ...), custom_call_target="tpu_custom_call" | custom-call | flops 33822867456 | bytes 12582912 | tf_op jit(solution)/shard_map/loss_and_gradients/pallas_call | solution.py:490
  137.0 0.0 copy-start
  137.0 0.0 copy-start.1
  137.0 10.5 %adagrad_step.1 = (f32[4096,256]{1,0:T(8,128)}, f32[1,4096]{1,0:T(1,128)}) custom-call(bf16[4096,256]{1,0:T(8,128)(2,1)} %get-tuple-element.13.g_ref, f32[192,256]{1,0:T(8,128)} %get-tuple-element.14.negsum_ref, f32[4,128]{1,0:T(4,128)} %get-tuple-element.15.negid_ref, f32[4096,256]{1,0:T(8,128)} %table_ref.3, f32[1,4096]{1,0:T(1,128)} %bitcast.6), custom_call_target="tpu_custom_call" | custom-call | tf_op jit(solution)/shard_map/adagrad_step/pallas_call | solution.py:543
  147.5 0.0 copy-done
  147.5 0.8 copy.13
  148.3 0.0 copy-done.1
  148.3 0.6 copy.14
Async XLA Ops:
  137.0 10.5 %copy-start = (bf16[1024,256]{1,0:T(8,128)(2,1)S(1)}, bf16[1024,256]{1,0:T(8,128)(2,1)}, u32[]{:S(2)}) copy-start(bf16[1024,256]{1,0:T(8,128)(2,1)} %get-tuple-element.22) | copy-start | bytes 1572868
  137.0 11.3 %copy-start.1 = (f32[1,1024]{1,0:T(1,128)S(1)}, f32[1,1024]{1,0:T(1,128)}, u32[]{:S(2)}) copy-start(f32[1,1024]{1,0:T(1,128)} %get-tuple-element.12) | copy-start | bytes 12292

commit v2 on v1

v2 whole, which is shorter than its diff:
```python
import functools

import jax
import jax.numpy as jnp
from jax import lax
from jax.experimental import pallas as pl
from jax.experimental.pallas import tpu as pltpu
from jax.sharding import PartitionSpec as P

INV_TEMP = 20.0
LEARN_RATE = 0.05
EPSILON = 1e-06
LOG2E = 1.4426950408889634
BF, F32 = jnp.bfloat16, jnp.float32
LANES = 128


def dot(a, b):
    return jnp.dot(a, b, preferred_element_type=F32)


def iota(shape, dim):
    return lax.broadcasted_iota(jnp.int32, shape, dim).astype(F32)


def eye():
    return lax.broadcasted_iota(jnp.int32, (LANES, LANES), 0) == lax.broadcasted_iota(jnp.int32, (LANES, LANES), 1)


def row_to_col(row):
    parts = []
    for k in range(row.shape[1] // LANES):
        wide = jnp.broadcast_to(row[:, k * LANES : (k + 1) * LANES], (LANES, LANES))
        parts.append(jnp.sum(jnp.where(eye(), wide, 0.0), axis=1, keepdims=True))
    return parts[0] if len(parts) == 1 else jnp.concatenate(parts, axis=0)


def col_to_row(col):
    parts = []
    for k in range(col.shape[0] // LANES):
        wide = jnp.broadcast_to(col[k * LANES : (k + 1) * LANES], (LANES, LANES))
        parts.append(jnp.sum(jnp.where(eye(), wide, 0.0), axis=0, keepdims=True))
    return parts[0] if len(parts) == 1 else jnp.concatenate(parts, axis=1)


def pick_lanes(col, first, count):
    return (col == iota((col.shape[0], count), 1) + first).astype(BF)


def pick_rows(row, first, count):
    return (row == iota((count, row.shape[1]), 0) + first).astype(BF)


OFFSETS = (
    (1, 2), (3, 2), (2, 1), (2, 3), (1, 1), (3, 3), (1, 3), (3, 1),
    (2, 2), (2, 0), (0, 2), (0, 0), (0, 1), (0, 3), (1, 0), (3, 0),
)


def main_kernel(
    n_dp, n_item,
    neg_s_ref, q_ref, table_hbm, state_ref, owner_ref, row_ref, neg_ref,
    grad_ref, loss_ref, table_out, state_out,
    table_ref, neg_f, tsend, qt, req_out, req_in, negbuf, nidbuf, found, returned, outbox, inbox, acc, pos_f, ut, tot, et, part, sib_in, red_in, red_out, y_in,
    dense_f, rs_out, relay_in, rs_in, ag,
    req_s, req_r, neg_s, neg_r, nid_s, nid_r, pc_s, pc_r, pi_s, pi_r, sn_s, sn_r, si_s, si_r, pos_s, pos_r, g_s, g_r, sib_s, sib_r, red_s, red_r, y_s, y_r,
    rs_s, relay_r, rs_r, ag_s, ag_r, load_s, store_s,
):
    ex, width = q_ref.shape
    rows = table_ref.shape[0]
    quarter = rows // n_dp
    hq = quarter // 2
    chips = n_item // 2
    cap = 3 * ex // n_item
    neg = negbuf.shape[2]
    y, me = lax.axis_index("dp"), lax.axis_index("item")
    chip, core = me // 2, lax.rem(me, 2)
    sibling = chip * 2 + 1 - core
    up, far, down = lax.rem(y + 1, n_dp), lax.rem(y + 2, n_dp), lax.rem(y + 3, n_dp)

    def copy(src, dst, send, recv, **where):
        return pltpu.make_async_remote_copy(
            src_ref=src, dst_ref=dst, send_sem=send, recv_sem=recv, device_id=where, device_id_type=pl.DeviceIdType.MESH
        )

    def load(k):
        at = pl.ds(pl.multiple_of(k * hq, hq), hq)
        return pltpu.make_async_copy(table_hbm.at[at, :], table_ref.at[at, :], load_s.at[k])

    def store(k):
        at = pl.ds(pl.multiple_of(k * hq, hq), hq)
        return pltpu.make_async_copy(table_ref.at[at, :], table_out.at[at, :], store_s.at[k])

    @pl.loop(0, 2 * n_dp)
    def _(k):
        load(k).start()

    barrier = pltpu.get_barrier_semaphore()

    @pl.loop(1, n_item)
    def _(off):
        pl.semaphore_signal(barrier, inc=1, device_id={"item": lax.rem(me + off, n_item)}, device_id_type=pl.DeviceIdType.MESH)

    @pl.loop(1, n_dp)
    def _(off):
        pl.semaphore_signal(barrier, inc=1, device_id={"dp": lax.rem(y + off, n_dp)}, device_id_type=pl.DeviceIdType.MESH)

    owner_r = owner_ref[...].astype(F32)
    row_r = row_ref[...].astype(F32)
    gid_r = owner_r * rows + row_r
    owners_r = (owner_r == iota((n_item, ex), 0)).astype(F32)
    before = (iota((LANES, LANES), 0) < iota((LANES, LANES), 1)).astype(BF)
    seen = jnp.zeros((n_item, 1), F32)
    slots = []
    for k in range(ex // LANES):
        named = owners_r[:, k * LANES : (k + 1) * LANES]
        earlier = dot(named.astype(BF), before) + seen
        slots.append(jnp.sum(earlier * named, axis=0, keepdims=True))
        seen += jnp.sum(named, axis=1, keepdims=True)
    slot_r = jnp.concatenate(slots, axis=1)
    place_r = owner_r * cap + slot_r
    high_r = jnp.floor(row_r * (1.0 / 64.0))
    low_r = row_r - 64.0 * high_r
    at_slot = slot_r == iota((LANES, ex), 0)
    both = jnp.concatenate([jnp.where(at_slot, high_r, 0.0), jnp.where(at_slot, low_r, 0.0)], axis=0).astype(BF)
    asked2 = lax.dot_general(owners_r.astype(BF), both, (((1,), (1,)), ((), ())), preferred_element_type=F32)
    asked = asked2[:, :LANES] * 64.0 + asked2[:, LANES:]
    for s in range(n_item):
        req_out[s] = asked[s : s + 1, :]

    pl.semaphore_wait(barrier, n_item - 1 + n_dp - 1)

    req_in[me] = req_out[me]

    def req_copy(peer):
        return copy(req_out.at[peer], req_in.at[me], req_s.at[peer], req_r.at[me], item=peer)

    @pl.loop(1, n_item)
    def _(off):
        req_copy(lax.rem(me + off, n_item)).start()

    @pl.loop(0, 2 * n_dp)
    def _(k):
        load(k).wait()

    for k in range(neg):
        neg_f[k : k + 1, :] = table_ref[pl.ds(neg_s_ref[k], 1), :]
    t = neg_f[...]
    mine = y * 2 + core
    negbuf[mine, chip] = (t / jnp.sqrt(jnp.sum(t * t, axis=1, keepdims=True) + EPSILON)).astype(BF)
    nidbuf[mine, chip] = jnp.concatenate([neg_ref[...].astype(F32), jnp.full((1, LANES - neg), -1.0, F32)], axis=1)

    def plane_copies(peer_chip):
        to = peer_chip * 2 + core
        return (
            copy(negbuf.at[mine, chip], negbuf.at[mine, chip], neg_s.at[peer_chip], neg_r.at[chip], item=to),
            copy(nidbuf.at[mine, chip], nidbuf.at[mine, chip], nid_s.at[peer_chip], nid_r.at[chip], item=to),
        )

    @pl.loop(1, chips)
    def _(off):
        for c in plane_copies(lax.rem(chip + off, chips)):
            c.start()

    tile = min(512, rows)

    @pl.loop(0, rows // tile)
    def _(k):
        at = pl.ds(pl.multiple_of(k * tile, tile), tile)
        t = table_ref[at, :]
        tsend[at, :] = (t / jnp.sqrt(jnp.sum(t * t, axis=1, keepdims=True) + EPSILON)).astype(BF)

    q = q_ref[...].astype(F32)
    q_norm = jnp.sqrt(jnp.sum(q * q, axis=1, keepdims=True) + EPSILON)
    acc[...] = q / q_norm
    qt[...] = jnp.transpose(acc[...]).astype(BF)

    def wait_recv(dst, send, recv, **where):
        copy(dst, dst, send, recv, **where).wait_recv()

    @pl.loop(1, n_item)
    def _(off):
        src = lax.rem(me + off, n_item)
        wait_recv(req_in.at[src], req_s.at[src], req_r.at[src], item=src)

    if chips == len(OFFSETS):
        order = [lax.rem(chip // 4 + dz, 4) * 4 + lax.rem(chip + dx, 4) for dz, dx in OFFSETS]
    else:
        order = [lax.rem(chip + d, chips) for d in range(1, chips + 1)]
    mates = [2 * c + side for c in order for side in range(2)]
    batch = min(8, n_item)
    batches = [mates[k : k + batch] for k in range(0, n_item, batch)]

    def pos_copy(peer):
        return copy(found.at[peer], returned.at[me], pos_s.at[peer], pos_r.at[me], item=peer)

    def gather(group):
        ids = jnp.concatenate([row_to_col(req_in[src])[:cap] for src in group], axis=0)
        got = jnp.zeros((batch * cap, width), F32)
        for t in range(rows // tile):
            got += dot(pick_lanes(ids, float(t * tile), tile), tsend[t * tile : (t + 1) * tile, :])
        for s, src in enumerate(group):
            found[src] = got[s * cap : (s + 1) * cap].astype(BF)

            @pl.when(src != me)
            def _():
                pos_copy(src).start()

    gather(batches[0])

    @pl.loop(1, chips)
    def _(off):
        src = lax.rem(chip + off, chips)
        wait_recv(negbuf.at[mine, src], neg_s.at[src], neg_r.at[src], item=src * 2 + core)
        wait_recv(nidbuf.at[mine, src], nid_s.at[src], nid_r.at[src], item=src * 2 + core)

    half = chips // 2

    def piece_part(d, h):
        return negbuf.at[d * 2 + core, pl.ds(h * half, half)], nidbuf.at[d * 2 + core, pl.ds(h * half, half)]

    def y_copies(d, h, way, dest):
        rows_part, ids_part = piece_part(d, h)
        return (
            copy(rows_part, rows_part, pc_s.at[way, h], pc_r.at[d, h], dp=dest),
            copy(ids_part, ids_part, pi_s.at[way, h], pi_r.at[d, h], dp=dest),
        )

    def y_wait(d, h, dest):
        for c in y_copies(d, h, 0, dest):
            c.wait_recv()

    def sib_copies(d, side):
        piece = d * 2 + side
        return (
            copy(negbuf.at[piece], negbuf.at[piece], sn_s.at[d], sn_r.at[d], item=sibling),
            copy(nidbuf.at[piece], nidbuf.at[piece], si_s.at[d], si_r.at[d], item=sibling),
        )

    def to_sibling(d):
        for c in sib_copies(d, core):
            c.start()

    def from_sibling(d):
        for c in sib_copies(d, 1 - core):
            c.wait_recv()

    def send_y(d, h, way, dest):
        for c in y_copies(d, h, way, dest):
            c.start()

    send_y(y, 0, 0, up)
    send_y(y, 1, 1, down)
    send_y(y, 1, 0, up)
    send_y(y, 0, 1, down)
    to_sibling(y)

    for group in batches[1:]:
        gather(group)

    returned[me] = found[me]

    tot[...] = jnp.zeros_like(tot)

    def pass1(piece):
        @pl.loop(0, chips // half)
        def _(h):
            first = h * half
            block = negbuf[piece, pl.ds(first, half)].reshape(half * neg, width)
            ids = jnp.concatenate(
                [
                    row_to_col(nidbuf[piece, first + z])[:neg]
                    + (((first + z) * 2 + lax.rem(piece, 2)) * rows).astype(F32)
                    for z in range(half)
                ],
                axis=0,
            )
            e = jnp.where(ids != gid_r, jnp.exp2(dot(block, qt[...]) * (INV_TEMP * LOG2E)), 0.0)
            tot[...] += jnp.sum(e.reshape(half * neg // 8, 8, ex), axis=0)
            eb = e.astype(BF)
            et[piece, pl.ds(first, half)] = eb.reshape(half, neg, ex)

    from_sibling(y)

    @pl.loop(0, 2)
    def _(side):
        pass1(y * 2 + side)

    y_wait(down, 0, down)
    send_y(down, 0, 2, up)
    y_wait(up, 1, up)
    send_y(up, 1, 2, down)
    y_wait(down, 1, down)
    to_sibling(down)
    y_wait(up, 0, up)
    to_sibling(up)

    @pl.loop(0, 2)
    def _(k):
        pass1(lax.rem(y + 1 + 2 * k, n_dp) * 2 + core)

    from_sibling(down)
    from_sibling(up)

    @pl.loop(0, 2)
    def _(k):
        pass1(lax.rem(y + 1 + 2 * k, n_dp) * 2 + 1 - core)

    y_wait(far, 0, down)
    y_wait(far, 1, up)
    to_sibling(far)
    pass1(far * 2 + core)
    from_sibling(far)
    pass1(far * 2 + 1 - core)

    @pl.loop(1, n_item)
    def _(off):
        src = lax.rem(me + off, n_item)
        wait_recv(returned.at[src], pos_s.at[src], pos_r.at[src], item=src)

    q_hat = acc[...]
    place_c = row_to_col(place_r)
    pos_e = jnp.zeros((ex, width), F32)
    for k in range(0, n_item, batch):
        pick = pick_lanes(place_c, float(k * cap), batch * cap)
        pos_e += dot(pick, returned[k : k + batch].reshape(batch * cap, width))
    pos_f[...] = pos_e
    s_pos = INV_TEMP * jnp.sum(q_hat.astype(BF).astype(F32) * pos_e, axis=1, keepdims=True)
    neg_tot = row_to_col(jnp.sum(tot[...], axis=0, keepdims=True))
    lse = jnp.log(jnp.exp(s_pos) + neg_tot)
    loss_ref[...] = col_to_row(lse - s_pos)
    coef = jnp.exp(s_pos - lse) - 1.0
    inv_tot = jnp.exp(-lse)

    g_pos = (INV_TEMP * coef * q_hat).astype(BF)

    def g_copy(peer):
        return copy(outbox.at[peer], inbox.at[me], g_s.at[peer], g_r.at[me], item=peer)

    for group in batches:
        wanted = jnp.concatenate([iota((cap, 1), 0) + (src * cap).astype(F32) for src in group], axis=0)
        rows_out = dot((place_r == wanted).astype(BF), g_pos)
        for s, src in enumerate(group):
            outbox[src] = rows_out[s * cap : (s + 1) * cap].astype(BF)

            @pl.when(src != me)
            def _():
                g_copy(src).start()

    inbox[me] = outbox[me]

    q_scaled = (q_hat.astype(BF).astype(F32) * (INV_TEMP * inv_tot)).astype(BF)

    def pass2(side):
        @pl.loop(0, n_dp)
        def _(d):
            for h in range(chips // half):
                at = slice(h * half, (h + 1) * half)
                p = dot(et[d * 2 + side, at].reshape(half * neg, ex), q_scaled)
                p = p.astype(BF).reshape(half, neg, width)
                for z in range(half):
                    part[side, h * half + z, pl.ds(pl.multiple_of(d * neg, neg), neg), :] = p[z]

    pass2(1 - core)
    to_sib = copy(part.at[1 - core], sib_in, sib_s, sib_r, item=sibling)
    to_sib.start()
    pass2(core)

    to_sib.wait_recv()

    @pl.loop(0, chips)
    def _(z):
        red_out[z] = (part[core, z].astype(F32) + sib_in[z].astype(F32)).astype(BF)

    def red_copy(peer_chip):
        return copy(red_out.at[peer_chip], red_in.at[chip], red_s.at[peer_chip], red_r.at[chip], item=peer_chip * 2 + core)

    for k, group in enumerate(batches):
        for src in group:

            @pl.when(src != me)
            def _():
                wait_recv(inbox.at[src], g_s.at[src], g_r.at[src], item=src)

        if k == len(batches) - 1:
            @pl.loop(1, chips)
            def _(off):
                red_copy(lax.rem(chip + off, chips)).start()

        ids = jnp.concatenate([req_in[src][:, :cap] for src in group], axis=1)
        came = jnp.concatenate([inbox[src] for src in group], axis=0)

        @pl.loop(0, n_dp)
        def _(d):
            at = pl.ds(pl.multiple_of(d * quarter, quarter), quarter)
            new = dot(pick_rows(ids, (d * quarter).astype(F32), quarter), came)
            if k == 0:
                dense_f[at, :] = new
            else:
                dense_f[at, :] += new

    def rs_copies():
        return (
            copy(rs_out.at[0, 0], relay_in.at[0], rs_s.at[0, 0], relay_r.at[0], dp=up),
            copy(rs_out.at[0, 1], relay_in.at[1], rs_s.at[0, 1], relay_r.at[1], dp=down),
            copy(rs_out.at[1, 0], rs_in.at[0, 0], rs_s.at[1, 0], rs_r.at[0, 0], dp=up),
            copy(rs_out.at[1, 1], rs_in.at[0, 1], rs_s.at[1, 1], rs_r.at[0, 1], dp=up),
            copy(rs_out.at[2, 0], rs_in.at[1, 0], rs_s.at[2, 0], rs_r.at[1, 0], dp=down),
            copy(rs_out.at[2, 1], rs_in.at[1, 1], rs_s.at[2, 1], rs_r.at[1, 1], dp=down),
        )

    def dense_part(d, h):
        return dense_f[pl.ds(pl.multiple_of(d * quarter + h * hq, hq), hq), :]

    far0, far1, up0, up1, down0, down1 = rs_copies()
    rs_out[0, 0] = dense_part(far, 0).astype(BF)
    far0.start()
    rs_out[0, 1] = dense_part(far, 1).astype(BF)
    far1.start()
    rs_out[1, 1] = dense_part(up, 1).astype(BF)
    up1.start()
    rs_out[2, 0] = dense_part(down, 0).astype(BF)
    down0.start()
    far0.wait_recv()
    rs_out[1, 0] = (dense_part(up, 0) + relay_in[0].astype(F32)).astype(BF)
    up0.start()
    far1.wait_recv()
    rs_out[2, 1] = (dense_part(down, 1) + relay_in[1].astype(F32)).astype(BF)
    down1.start()

    ut[...] = jnp.zeros_like(ut)

    @pl.loop(0, 2 * n_dp)
    def _(piece):
        block = negbuf[piece].reshape(chips * neg, width)
        eb = et[piece].reshape(chips * neg, ex)
        ut[...] += lax.dot_general(block, eb, (((0,), (0,)), ((), ())), preferred_element_type=F32)

    g_q = INV_TEMP * (coef * pos_f[...] + jnp.transpose(ut[...]) * inv_tot)
    grad_ref[...] = ((g_q - acc[...] * jnp.sum(acc[...] * g_q, axis=1, keepdims=True)) / q_norm).astype(BF)

    up1.wait_recv()
    up0.wait_recv()
    down0.wait_recv()
    down1.wait_recv()
    for h in range(2):
        ag[y, h] = (dense_part(y, h) + rs_in[0, h].astype(F32) + rs_in[1, h].astype(F32)).astype(BF)

    def ag_copy(slot, h, way, dest):
        return copy(ag.at[slot, h], ag.at[slot, h], ag_s.at[way, h], ag_r.at[slot, h], dp=dest)

    for h in range(2):
        ag_copy(y, h, 0, up).start()
        ag_copy(y, h, 1, down).start()
    total = red_out[chip].astype(F32)

    def add_red(off, total):
        src = lax.rem(chip + off, chips)
        wait_recv(red_in.at[src], red_s.at[src], red_r.at[src], item=src * 2 + core)
        return total + red_in[src].astype(F32)

    total = lax.fori_loop(1, chips, add_red, total)
    y_in[y] = total.astype(BF)

    def sum_copy(dest):
        return copy(y_in.at[y], y_in.at[y], y_s.at[dest], y_r.at[y], dp=dest)

    @pl.loop(1, n_dp)
    def _(off):
        sum_copy(lax.rem(y + off, n_dp)).start()

    @pl.loop(1, n_dp)
    def _(off):
        src = lax.rem(y + off, n_dp)
        wait_recv(y_in.at[src], y_s.at[src], y_r.at[src], dp=src)

    sums = y_in[0].astype(F32)
    for d in range(1, n_dp):
        sums += y_in[d].astype(F32)
    sums_high = sums.astype(BF)
    sums_low = (sums - sums_high.astype(F32)).astype(BF)
    neg_ids = jnp.concatenate([nidbuf[d * 2 + core, chip][:, :neg] for d in range(n_dp)], axis=1)

    def step(d, h):
        first = d * quarter + h * hq
        at = pl.ds(pl.multiple_of(first, hq), hq)
        pick = (neg_ids == iota((hq, n_dp * neg), 0) + first.astype(F32)).astype(BF)
        g = ag[d, h].astype(F32) + dot(pick, sums_high) + dot(pick, sums_low)
        t = table_ref[at, :]
        norm = jnp.sqrt(jnp.sum(t * t, axis=1, keepdims=True) + EPSILON)
        unit = t / norm
        g_row = (g - unit * jnp.sum(unit * g, axis=1, keepdims=True)) / norm
        mean = jnp.sum(g_row * g_row, axis=1, keepdims=True) * (1.0 / width)
        new = state_ref[:, at] + col_to_row(mean)
        state_out[:, at] = new
        table_ref[at, :] = t - LEARN_RATE * g_row / jnp.sqrt(row_to_col(new))
        store(d * 2 + h).start()

    def step_both(d):
        @pl.loop(0, 2)
        def _(h):
            step(d, h)

    step_both(y)

    wait_recv(ag.at[down, 0], ag_s.at[0, 0], ag_r.at[down, 0], dp=down)
    ag_copy(down, 0, 2, up).start()
    wait_recv(ag.at[up, 1], ag_s.at[0, 1], ag_r.at[up, 1], dp=up)
    ag_copy(up, 1, 2, down).start()

    wait_recv(ag.at[down, 1], ag_s.at[0, 1], ag_r.at[down, 1], dp=down)
    wait_recv(ag.at[up, 0], ag_s.at[0, 0], ag_r.at[up, 0], dp=up)

    @pl.loop(0, 2)
    def _(k):
        step_both(lax.rem(y + 1 + 2 * k, n_dp))

    wait_recv(ag.at[far, 0], ag_s.at[0, 0], ag_r.at[far, 0], dp=down)
    wait_recv(ag.at[far, 1], ag_s.at[0, 1], ag_r.at[far, 1], dp=up)
    step_both(far)

    @pl.loop(1, n_item)
    def _(off):
        peer = lax.rem(me + off, n_item)
        req_copy(peer).wait_send()
        pos_copy(peer).wait_send()
        g_copy(peer).wait_send()

    @pl.loop(1, chips)
    def _(off):
        peer = lax.rem(chip + off, chips)
        for c in plane_copies(peer):
            c.wait_send()
        red_copy(peer).wait_send()

    @pl.loop(1, n_dp)
    def _(off):
        sum_copy(lax.rem(y + off, n_dp)).wait_send()

    @pl.loop(0, n_dp)
    def _(d):
        for c in sib_copies(d, core):
            c.wait_send()

    for h in range(2):
        for c in (*y_copies(y, h, 0, up), *y_copies(y, h, 1, down)):
            c.wait_send()
    for c in (*y_copies(down, 0, 2, up), *y_copies(up, 1, 2, down)):
        c.wait_send()

    to_sib.wait_send()
    for c in rs_copies():
        c.wait_send()
    for h in range(2):
        ag_copy(y, h, 0, up).wait_send()
        ag_copy(y, h, 1, down).wait_send()
    ag_copy(down, 0, 2, up).wait_send()
    ag_copy(up, 1, 2, down).wait_send()

    @pl.loop(0, 2 * n_dp)
    def _(k):
        store(k).wait()


def on_device(n_dp, n_item, queries, item_table, adagrad_state, pos_owner, pos_row, neg_rows):
    ex, width = queries.shape
    rows = item_table.shape[0]
    neg = neg_rows.shape[0]
    chips = n_item // 2
    cap = 3 * ex // n_item
    quarter = rows // n_dp
    vmem, hbm = pl.BlockSpec(memory_space=pltpu.VMEM), pl.BlockSpec(memory_space=pl.ANY)
    dma = pltpu.SemaphoreType.DMA
    n_neg = 2 * n_dp * chips * neg
    flops = 2 * width * (3 * n_neg * ex + 3 * n_item * cap * (rows + ex))
    grad, loss, new_table, new_state = pl.pallas_call(
        functools.partial(main_kernel, n_dp, n_item),
        out_shape=(
            jax.ShapeDtypeStruct((ex, width), BF),
            jax.ShapeDtypeStruct((1, ex), F32),
            jax.ShapeDtypeStruct((rows, width), F32),
            jax.ShapeDtypeStruct((1, rows), F32),
        ),
        in_specs=[pl.BlockSpec(memory_space=pltpu.SMEM), vmem, hbm, vmem, vmem, vmem, vmem],
        out_specs=(vmem, vmem, hbm, vmem),
        scratch_shapes=[
            pltpu.VMEM((rows, width), F32),
            pltpu.VMEM((neg, width), F32),
            pltpu.VMEM((rows, width), BF),
            pltpu.VMEM((width, ex), BF),
            pltpu.VMEM((n_item, 1, LANES), F32),
            pltpu.VMEM((n_item, 1, LANES), F32),
            pltpu.VMEM((2 * n_dp, chips, neg, width), BF),
            pltpu.VMEM((2 * n_dp, chips, 1, LANES), F32),
            pltpu.VMEM((n_item, cap, width), BF),
            pltpu.VMEM((n_item, cap, width), BF),
            pltpu.VMEM((n_item, cap, width), BF),
            pltpu.VMEM((n_item, cap, width), BF),
            pltpu.VMEM((ex, width), F32),
            pltpu.VMEM((ex, width), F32),
            pltpu.VMEM((width, ex), F32),
            pltpu.VMEM((8, ex), F32),
            pltpu.VMEM((2 * n_dp, chips, neg, ex), BF),
            pltpu.VMEM((2, chips, n_dp * neg, width), BF),
            pltpu.VMEM((chips, n_dp * neg, width), BF),
            pltpu.VMEM((chips, n_dp * neg, width), BF),
            pltpu.VMEM((chips, n_dp * neg, width), BF),
            pltpu.VMEM((n_dp, n_dp * neg, width), BF),
            pltpu.VMEM((rows, width), F32),
            pltpu.VMEM((3, 2, quarter // 2, width), BF),
            pltpu.VMEM((2, quarter // 2, width), BF),
            pltpu.VMEM((2, 2, quarter // 2, width), BF),
            pltpu.VMEM((n_dp, 2, quarter // 2, width), BF),
            dma((n_item,)), dma((n_item,)),
            dma((chips,)), dma((chips,)),
            dma((chips,)), dma((chips,)),
            dma((3, 2)), dma((n_dp, 2)),
            dma((3, 2)), dma((n_dp, 2)),
            dma((n_dp,)), dma((n_dp,)),
            dma((n_dp,)), dma((n_dp,)),
            dma((n_item,)), dma((n_item,)),
            dma((n_item,)), dma((n_item,)),
            dma, dma,
            dma((chips,)), dma((chips,)),
            dma((n_dp,)), dma((n_dp,)),
            dma((3, 2)), dma((2,)), dma((2, 2)),
            dma((3, 2)), dma((n_dp, 2)),
            dma((2 * n_dp,)), dma((2 * n_dp,)),
        ],
        compiler_params=pltpu.CompilerParams(collective_id=0, has_side_effects=True, vmem_limit_bytes=62 * 2**20),
        cost_estimate=pl.CostEstimate(flops=flops, bytes_accessed=12 * 2**20, transcendentals=n_neg * ex),
        name="training_step",
    )(
        neg_rows, queries, item_table, adagrad_state.reshape(1, rows), pos_owner.reshape(1, ex), pos_row.reshape(1, ex),
        neg_rows.reshape(1, neg),
    )
    return grad, loss.reshape(ex), new_table, new_state.reshape(rows)


def solution(mesh):
    both = ("dp", "item")
    return jax.shard_map(
        functools.partial(on_device, mesh.shape["dp"], mesh.shape["item"]),
        mesh=mesh,
        in_specs=(P(both, None), P("item", None), P("item"), P(both, None), P(both), P(both)),
        out_specs=(P(both, None), P(both), P("item", None), P("item")),
        check_vma=False,
    )
```

time: 150 us -> 134 us (0.89)
  Pallas kernels: 144 us -> 125 us
  local copies, waits for them, and re-layouts: 4.27 us -> 8.23 us
    pallas_call x1 -> x0, Pallas kernels: 10.5 us -> none  [on_device(): pl.pallas_call(step_kernel, grid=(rows // tile,), out_shape=(jax.ShapeDty...]
    pallas_call x1, Pallas kernels: 134 us -> 125 us  [on_device(): pl.pallas_call(functools.partial(main_kernel, n_dp, n_item), out_shape=(j...]
    unnamed x7 -> x6, local copies, waits for them, and re-layouts: 3.1 us -> 8.23 us
where the time goes in v2:
time: 134 us
  Pallas kernels  125 us (93%)
  local copies, waits for them, and re-layouts  8.23 us (6%)
    pallas_call x1, Pallas kernels, on_device(): pl.pallas_call(functools.partial(main_kernel, n_dp, n_item), out_shape=(j...  125 us
    unnamed x6, local copies, waits for them, and re-layouts  8.23 us

profile of v2, /device:TPU:1, one launch (start us, length us, event | category | flops | bytes accessed | tf_op | source)
XLA Modules:
  0.0 133.6 jit_solution(2802491346481841423)
XLA Ops:
  0.6 124.7 %training_step.1 = (bf16[1024,256]{1,0:T(8,128)(2,1)}, f32[1,1024]{1,0:T(1,128)}, f32[4096,256]{1,0:T(8,128)}, f32[1,4096]{1,0:T(1,128)}) custom-call(s32[48]{0:T(128)} %neg_s_ref.1, bf16[1024,256]{1,0:T(8,128)(2,1)} %q_ref.1, f32[4096,256]{1,0:T(8,128)} %table_hbm.1, f32[1,4096]{1,0:T(1,128)} %bitcast.8, s32[1,1024]{1,0:T(1,128)} %bitcast.9, ...), custom_call_target="tpu_custom_call" | custom-call | flops 33822867456 | bytes 12582912 | tf_op jit(solution)/shard_map/training_step/pallas_call | solution.py:576
  125.4 1.9 %copy.14 = bf16[1024,256]{1,0:T(8,128)(2,1)} copy(bf16[1024,256]{1,0:T(8,128)(2,1)} %get-tuple-element.16) | data formatting | bytes 1048576
  127.2 1.3 copy.15
  128.5 0.0 copy-start
  128.5 4.5 %copy.16 = f32[4096,256]{1,0:T(8,128)} copy(f32[4096,256]{1,0:T(8,128)} %get-tuple-element.18) | data formatting | bytes 8388608
  133.0 0.0 copy-done
  133.0 0.6 copy.17
Async XLA Ops:
  128.5 4.5 %copy-start = (f32[1,4096]{1,0:T(1,128)S(1)}, f32[1,4096]{1,0:T(1,128)}, u32[]{:S(2)}) copy-start(f32[1,4096]{1,0:T(1,128)} %get-tuple-element.11) | copy-start | bytes 49156

commit v3 on v2

--- a/solution.py
+++ b/solution.py
@@ -60,11 +60,11 @@
 def main_kernel(
     n_dp, n_item,
     neg_s_ref, q_ref, table_hbm, state_ref, owner_ref, row_ref, neg_ref,
-    grad_ref, loss_ref, table_out, state_out,
-    table_ref, neg_f, tsend, qt, req_out, req_in, negbuf, nidbuf, found, returned, outbox, inbox, acc, pos_f, ut, tot, et, part, sib_in, red_in, red_out, y_in,
+    grad_ref, loss_ref, table_ref, state_out,
+    neg_f, tsend, qt, req_out, req_in, negbuf, nidbuf, found, returned, outbox, inbox, acc, pos_f, g_bf, ut, tot, et, part, sib_in, red_in, red_out, y_in,
     dense_f, rs_out, relay_in, rs_in, ag,
     req_s, req_r, neg_s, neg_r, nid_s, nid_r, pc_s, pc_r, pi_s, pi_r, sn_s, sn_r, si_s, si_r, pos_s, pos_r, g_s, g_r, sib_s, sib_r, red_s, red_r, y_s, y_r,
-    rs_s, relay_r, rs_r, ag_s, ag_r, load_s, store_s,
+    rs_s, relay_r, rs_r, ag_s, ag_r, load_s,
 ):
     ex, width = q_ref.shape
     rows = table_ref.shape[0]
@@ -86,10 +86,6 @@
     def load(k):
         at = pl.ds(pl.multiple_of(k * hq, hq), hq)
         return pltpu.make_async_copy(table_hbm.at[at, :], table_ref.at[at, :], load_s.at[k])
-
-    def store(k):
-        at = pl.ds(pl.multiple_of(k * hq, hq), hq)
-        return pltpu.make_async_copy(table_ref.at[at, :], table_out.at[at, :], store_s.at[k])
 
     @pl.loop(0, 2 * n_dp)
     def _(k):
@@ -206,7 +202,16 @@
             def _():
                 pos_copy(src).start()
 
-    gather(batches[0])
+    def one_of(k):
+        group = batches[-1]
+        for n in range(len(batches) - 2, -1, -1):
+            group = [jnp.where(k == n, a, b) for a, b in zip(batches[n], group)]
+        return group
+
+    @pl.loop(0, 1)
+    def _(k):
+        gather(one_of(k))
+
 
     @pl.loop(1, chips)
     def _(off):
@@ -255,8 +260,9 @@
     send_y(y, 0, 1, down)
     to_sibling(y)
 
-    for group in batches[1:]:
-        gather(group)
+    @pl.loop(1, len(batches))
+    def _(k):
+        gather(one_of(k))
 
     returned[me] = found[me]
 
@@ -313,18 +319,27 @@
     from_sibling(far)
     pass1(far * 2 + 1 - core)
 
-    @pl.loop(1, n_item)
-    def _(off):
-        src = lax.rem(me + off, n_item)
-        wait_recv(returned.at[src], pos_s.at[src], pos_r.at[src], item=src)
+    place_c = row_to_col(place_r)
+    pos_f[...] = jnp.zeros_like(pos_f)
+
+    def slots_of(group):
+        first = lax.broadcasted_iota(jnp.int32, (1, cap), 1)
+        return jnp.concatenate([first + src * cap for src in group], axis=1).astype(F32)
+
+    @pl.loop(0, len(batches))
+    def _(k):
+        group = one_of(k)
+        for src in group:
+
+            @pl.when(src != me)
+            def _():
+                wait_recv(returned.at[src], pos_s.at[src], pos_r.at[src], item=src)
+
+        pick = (place_c == slots_of(group)).astype(BF)
+        pos_f[...] += dot(pick, jnp.concatenate([returned[src] for src in group], axis=0))
 
     q_hat = acc[...]
-    place_c = row_to_col(place_r)
-    pos_e = jnp.zeros((ex, width), F32)
-    for k in range(0, n_item, batch):
-        pick = pick_lanes(place_c, float(k * cap), batch * cap)
-        pos_e += dot(pick, returned[k : k + batch].reshape(batch * cap, width))
-    pos_f[...] = pos_e
+    pos_e = pos_f[...]
     s_pos = INV_TEMP * jnp.sum(q_hat.astype(BF).astype(F32) * pos_e, axis=1, keepdims=True)
     neg_tot = row_to_col(jnp.sum(tot[...], axis=0, keepdims=True))
     lse = jnp.log(jnp.exp(s_pos) + neg_tot)
@@ -332,14 +347,16 @@
     coef = jnp.exp(s_pos - lse) - 1.0
     inv_tot = jnp.exp(-lse)
 
-    g_pos = (INV_TEMP * coef * q_hat).astype(BF)
+    g_bf[...] = (INV_TEMP * coef * q_hat).astype(BF)
 
     def g_copy(peer):
         return copy(outbox.at[peer], inbox.at[me], g_s.at[peer], g_r.at[me], item=peer)
 
-    for group in batches:
+    @pl.loop(0, len(batches))
+    def _(k):
+        group = one_of(k)
         wanted = jnp.concatenate([iota((cap, 1), 0) + (src * cap).astype(F32) for src in group], axis=0)
-        rows_out = dot((place_r == wanted).astype(BF), g_pos)
+        rows_out = dot((place_r == wanted).astype(BF), g_bf[...])
         for s, src in enumerate(group):
             outbox[src] = rows_out[s * cap : (s + 1) * cap].astype(BF)
 
@@ -375,17 +392,16 @@
     def red_copy(peer_chip):
         return copy(red_out.at[peer_chip], red_in.at[chip], red_s.at[peer_chip], red_r.at[chip], item=peer_chip * 2 + core)
 
+    @pl.loop(1, chips)
+    def _(off):
+        red_copy(lax.rem(chip + off, chips)).start()
+
     for k, group in enumerate(batches):
         for src in group:
 
             @pl.when(src != me)
             def _():
                 wait_recv(inbox.at[src], g_s.at[src], g_r.at[src], item=src)
-
-        if k == len(batches) - 1:
-            @pl.loop(1, chips)
-            def _(off):
-                red_copy(lax.rem(chip + off, chips)).start()
 
         ids = jnp.concatenate([req_in[src][:, :cap] for src in group], axis=1)
         came = jnp.concatenate([inbox[src] for src in group], axis=0)
@@ -439,6 +455,48 @@
     g_q = INV_TEMP * (coef * pos_f[...] + jnp.transpose(ut[...]) * inv_tot)
     grad_ref[...] = ((g_q - acc[...] * jnp.sum(acc[...] * g_q, axis=1, keepdims=True)) / q_norm).astype(BF)
 
+    @pl.loop(1, n_item)
+    def _(off):
+        peer = lax.rem(me + off, n_item)
+        req_copy(peer).wait_send()
+        pos_copy(peer).wait_send()
+        g_copy(peer).wait_send()
+
+    @pl.loop(1, chips)
+    def _(off):
+        peer = lax.rem(chip + off, chips)
+        for c in plane_copies(peer):
+            c.wait_send()
+        red_copy(peer).wait_send()
+
+    @pl.loop(0, n_dp)
+    def _(d):
+        for c in sib_copies(d, core):
+            c.wait_send()
+
+    for h in range(2):
+        for c in (*y_copies(y, h, 0, up), *y_copies(y, h, 1, down)):
+            c.wait_send()
+    for c in (*y_copies(down, 0, 2, up), *y_copies(up, 1, 2, down)):
+        c.wait_send()
+
+    total = red_out[chip].astype(F32)
+
+    def add_red(off, total):
+        src = lax.rem(chip + off, chips)
+        wait_recv(red_in.at[src], red_s.at[src], red_r.at[src], item=src * 2 + core)
+        return total + red_in[src].astype(F32)
+
+    total = lax.fori_loop(1, chips, add_red, total)
+    y_in[y] = total.astype(BF)
+
+    def sum_copy(dest):
+        return copy(y_in.at[y], y_in.at[y], y_s.at[dest], y_r.at[y], dp=dest)
+
+    @pl.loop(1, n_dp)
+    def _(off):
+        sum_copy(lax.rem(y + off, n_dp)).start()
+
     up1.wait_recv()
     up0.wait_recv()
     down0.wait_recv()
@@ -452,23 +510,6 @@
     for h in range(2):
         ag_copy(y, h, 0, up).start()
         ag_copy(y, h, 1, down).start()
-    total = red_out[chip].astype(F32)
-
-    def add_red(off, total):
-        src = lax.rem(chip + off, chips)
-        wait_recv(red_in.at[src], red_s.at[src], red_r.at[src], item=src * 2 + core)
-        return total + red_in[src].astype(F32)
-
-    total = lax.fori_loop(1, chips, add_red, total)
-    y_in[y] = total.astype(BF)
-
-    def sum_copy(dest):
-        return copy(y_in.at[y], y_in.at[y], y_s.at[dest], y_r.at[y], dp=dest)
-
-    @pl.loop(1, n_dp)
-    def _(off):
-        sum_copy(lax.rem(y + off, n_dp)).start()
-
     @pl.loop(1, n_dp)
     def _(off):
         src = lax.rem(y + off, n_dp)
@@ -494,7 +535,6 @@
         new = state_ref[:, at] + col_to_row(mean)
         state_out[:, at] = new
         table_ref[at, :] = t - LEARN_RATE * g_row / jnp.sqrt(row_to_col(new))
-        store(d * 2 + h).start()
 
     def step_both(d):
         @pl.loop(0, 2)
@@ -519,34 +559,9 @@
     wait_recv(ag.at[far, 1], ag_s.at[0, 1], ag_r.at[far, 1], dp=up)
     step_both(far)
 
-    @pl.loop(1, n_item)
-    def _(off):
-        peer = lax.rem(me + off, n_item)
-        req_copy(peer).wait_send()
-        pos_copy(peer).wait_send()
-        g_copy(peer).wait_send()
-
-    @pl.loop(1, chips)
-    def _(off):
-        peer = lax.rem(chip + off, chips)
-        for c in plane_copies(peer):
-            c.wait_send()
-        red_copy(peer).wait_send()
-
     @pl.loop(1, n_dp)
     def _(off):
         sum_copy(lax.rem(y + off, n_dp)).wait_send()
-
-    @pl.loop(0, n_dp)
-    def _(d):
-        for c in sib_copies(d, core):
-            c.wait_send()
-
-    for h in range(2):
-        for c in (*y_copies(y, h, 0, up), *y_copies(y, h, 1, down)):
-            c.wait_send()
-    for c in (*y_copies(down, 0, 2, up), *y_copies(up, 1, 2, down)):
-        c.wait_send()
 
     to_sib.wait_send()
     for c in rs_copies():
@@ -556,10 +571,6 @@
         ag_copy(y, h, 1, down).wait_send()
     ag_copy(down, 0, 2, up).wait_send()
     ag_copy(up, 1, 2, down).wait_send()
-
-    @pl.loop(0, 2 * n_dp)
-    def _(k):
-        store(k).wait()
 
 
 def on_device(n_dp, n_item, queries, item_table, adagrad_state, pos_owner, pos_row, neg_rows):
@@ -576,15 +587,14 @@
     grad, loss, new_table, new_state = pl.pallas_call(
         functools.partial(main_kernel, n_dp, n_item),
         out_shape=(
-            jax.ShapeDtypeStruct((ex, width), BF),
-            jax.ShapeDtypeStruct((1, ex), F32),
-            jax.ShapeDtypeStruct((rows, width), F32),
-            jax.ShapeDtypeStruct((1, rows), F32),
+            pltpu.VMEM((ex, width), BF),
+            pltpu.VMEM((1, ex), F32),
+            pltpu.VMEM((rows, width), F32),
+            pltpu.VMEM((1, rows), F32),
         ),
         in_specs=[pl.BlockSpec(memory_space=pltpu.SMEM), vmem, hbm, vmem, vmem, vmem, vmem],
-        out_specs=(vmem, vmem, hbm, vmem),
+        out_specs=(vmem, vmem, vmem, vmem),
         scratch_shapes=[
-            pltpu.VMEM((rows, width), F32),
             pltpu.VMEM((neg, width), F32),
             pltpu.VMEM((rows, width), BF),
             pltpu.VMEM((width, ex), BF),
@@ -598,6 +608,7 @@
             pltpu.VMEM((n_item, cap, width), BF),
             pltpu.VMEM((ex, width), F32),
             pltpu.VMEM((ex, width), F32),
+            pltpu.VMEM((ex, width), BF),
             pltpu.VMEM((width, ex), F32),
             pltpu.VMEM((8, ex), F32),
             pltpu.VMEM((2 * n_dp, chips, neg, ex), BF),
@@ -625,9 +636,9 @@
             dma((n_dp,)), dma((n_dp,)),
             dma((3, 2)), dma((2,)), dma((2, 2)),
             dma((3, 2)), dma((n_dp, 2)),
-            dma((2 * n_dp,)), dma((2 * n_dp,)),
+            dma((2 * n_dp,)),
         ],
-        compiler_params=pltpu.CompilerParams(collective_id=0, has_side_effects=True, vmem_limit_bytes=62 * 2**20),
+        compiler_params=pltpu.CompilerParams(collective_id=0, has_side_effects=True, vmem_limit_bytes=56 * 2**20),
         cost_estimate=pl.CostEstimate(flops=flops, bytes_accessed=12 * 2**20, transcendentals=n_neg * ex),
         name="training_step",
     )(

time: 134 us -> 120 us (0.90)
  Pallas kernels: 125 us -> 114 us
  local copies, waits for them, and re-layouts: 8.23 us -> 4.01 us
    pallas_call x1, Pallas kernels: 125 us -> 114 us  [on_device(): pl.pallas_call(functools.partial(main_kernel, n_dp, n_item), out_shape=(p...]
    unnamed x6 -> x4, local copies, waits for them, and re-layouts: 8.23 us -> 4.01 us
where the time goes in v3:
time: 120 us; the launch traced here: 119 us
  Pallas kernels  114 us (95%)
  local copies, waits for them, and re-layouts  4.01 us (3%)
    pallas_call x1, Pallas kernels, on_device(): pl.pallas_call(functools.partial(main_kernel, n_dp, n_item), out_shape=(p...  114 us
    unnamed x4, local copies, waits for them, and re-layouts  4.01 us

profile of v3, /device:TPU:1, one launch (start us, length us, event | category | flops | bytes accessed | tf_op | source)
XLA Modules:
  0.0 118.9 jit_solution(1410882720772503490)
XLA Ops:
  0.6 114.2 %training_step.1 = (bf16[1024,256]{1,0:T(8,128)(2,1)S(1)}, f32[1,1024]{1,0:T(1,128)S(1)}, f32[4096,256]{1,0:T(8,128)S(1)}, f32[1,4096]{1,0:T(1,128)S(1)}) custom-call(s32[48]{0:T(128)} %neg_s_ref.1, bf16[1024,256]{1,0:T(8,128)(2,1)} %q_ref.1, f32[4096,256]{1,0:T(8,128)} %table_hbm.1, f32[1,4096]{1,0:T(1,128)} %bitcast.8, s32[1,1024]{1,0:T(1,128)} %bitcast.9, ...), custom_call_target="tpu_custom_call" | custom-call | flops 33822867456 | bytes 12582912 | tf_op jit(solution)/shard_map/training_step/pallas_call | solution.py:587
  114.9 0.8 copy.14
  115.7 0.6 copy.15
  116.2 0.6 copy.17
  116.9 2.0 %copy.16 = f32[4096,256]{1,0:T(8,128)} copy(f32[4096,256]{1,0:T(8,128)S(1)} %get-tuple-element.14) | data formatting | bytes 8388608

commit v4 on v3

--- a/solution.py
+++ b/solution.py
@@ -1,4 +1,5 @@
 import functools
+import math
 
 import jax
 import jax.numpy as jnp
@@ -61,9 +62,9 @@
     n_dp, n_item,
     neg_s_ref, q_ref, table_hbm, state_ref, owner_ref, row_ref, neg_ref,
     grad_ref, loss_ref, table_ref, state_out,
-    neg_f, tsend, qt, req_out, req_in, negbuf, nidbuf, found, returned, outbox, inbox, acc, pos_f, g_bf, ut, tot, et, part, sib_in, red_in, red_out, y_in,
+    neg_f, tsend, qt, req_out, req_in, negbuf, nidbuf, found, returned, outbox, inbox, acc, pos_f, g_bf, ut, tot, et, part, sib_in, by_x, by_z, in_x, in_z, mid_x, mid_z, end_x, end_z, y_out, y_in, y_sum,
     dense_f, rs_out, relay_in, rs_in, ag,
-    req_s, req_r, neg_s, neg_r, nid_s, nid_r, pc_s, pc_r, pi_s, pi_r, sn_s, sn_r, si_s, si_r, pos_s, pos_r, g_s, g_r, sib_s, sib_r, red_s, red_r, y_s, y_r,
+    req_s, req_r, neg_s, neg_r, nid_s, nid_r, pc_s, pc_r, pi_s, pi_r, sn_s, sn_r, si_s, si_r, pos_s, pos_r, g_s, g_r, sib_s, sib_r, hop_s, hop_r, y_s, y_r,
     rs_s, relay_r, rs_r, ag_s, ag_r, load_s,
 ):
     ex, width = q_ref.shape
@@ -85,11 +86,18 @@
 
     def load(k):
         at = pl.ds(pl.multiple_of(k * hq, hq), hq)
-        return pltpu.make_async_copy(table_hbm.at[at, :], table_ref.at[at, :], load_s.at[k])
+        return pltpu.make_async_copy(table_hbm.at[at, :], table_ref.at[at, :], load_s)
 
     @pl.loop(0, 2 * n_dp)
     def _(k):
         load(k).start()
+
+    def wait_all(part, send=None, recv=None):
+        c = copy(part, part, recv if send is None else send, send if recv is None else recv, item=sibling)
+        if send is None:
+            c.wait_recv()
+        else:
+            c.wait_send()
 
     barrier = pltpu.get_barrier_semaphore()
 
@@ -129,15 +137,13 @@
     req_in[me] = req_out[me]
 
     def req_copy(peer):
-        return copy(req_out.at[peer], req_in.at[me], req_s.at[peer], req_r.at[me], item=peer)
+        return copy(req_out.at[peer], req_in.at[me], req_s, req_r, item=peer)
 
     @pl.loop(1, n_item)
     def _(off):
         req_copy(lax.rem(me + off, n_item)).start()
 
-    @pl.loop(0, 2 * n_dp)
-    def _(k):
-        load(k).wait()
+    pltpu.make_async_copy(table_hbm, table_ref, load_s).wait()
 
     for k in range(neg):
         neg_f[k : k + 1, :] = table_ref[pl.ds(neg_s_ref[k], 1), :]
@@ -149,8 +155,8 @@
     def plane_copies(peer_chip):
         to = peer_chip * 2 + core
         return (
-            copy(negbuf.at[mine, chip], negbuf.at[mine, chip], neg_s.at[peer_chip], neg_r.at[chip], item=to),
-            copy(nidbuf.at[mine, chip], nidbuf.at[mine, chip], nid_s.at[peer_chip], nid_r.at[chip], item=to),
+            copy(negbuf.at[mine, chip], negbuf.at[mine, chip], neg_s, neg_r, item=to),
+            copy(nidbuf.at[mine, chip], nidbuf.at[mine, chip], nid_s, nid_r, item=to),
         )
 
     @pl.loop(1, chips)
@@ -174,10 +180,7 @@
     def wait_recv(dst, send, recv, **where):
         copy(dst, dst, send, recv, **where).wait_recv()
 
-    @pl.loop(1, n_item)
-    def _(off):
-        src = lax.rem(me + off, n_item)
-        wait_recv(req_in.at[src], req_s.at[src], req_r.at[src], item=src)
+    wait_all(req_in.at[pl.ds(0, n_item - 1)], recv=req_r)
 
     if chips == len(OFFSETS):
         order = [lax.rem(chip // 4 + dz, 4) * 4 + lax.rem(chip + dx, 4) for dz, dx in OFFSETS]
@@ -187,10 +190,28 @@
     batch = min(8, n_item)
     batches = [mates[k : k + batch] for k in range(0, n_item, batch)]
 
-    def pos_copy(peer):
-        return copy(found.at[peer], returned.at[me], pos_s.at[peer], pos_r.at[me], item=peer)
-
-    def gather(group):
+    def one_of(k):
+        group = batches[-1]
+        for n in range(len(batches) - 2, -1, -1):
+            group = [jnp.where(k == n, a, b) for a, b in zip(batches[n], group)]
+        return group
+
+    own_batch = (OFFSETS.index((0, 0)) if chips == len(OFFSETS) else chips - 1) * 2 // batch
+
+    def wait_batch(k, buffer, recv):
+        @pl.when(k != own_batch)
+        def _():
+            wait_all(buffer.at[pl.ds(0, batch)], recv=recv.at[k])
+
+        @pl.when(k == own_batch)
+        def _():
+            wait_all(buffer.at[pl.ds(0, batch - 1)], recv=recv.at[k])
+
+    def pos_copy(peer, k):
+        return copy(found.at[peer], returned.at[me], pos_s, pos_r.at[k], item=peer)
+
+    def gather(k):
+        group = one_of(k)
         ids = jnp.concatenate([row_to_col(req_in[src])[:cap] for src in group], axis=0)
         got = jnp.zeros((batch * cap, width), F32)
         for t in range(rows // tile):
@@ -200,46 +221,37 @@
 
             @pl.when(src != me)
             def _():
-                pos_copy(src).start()
-
-    def one_of(k):
-        group = batches[-1]
-        for n in range(len(batches) - 2, -1, -1):
-            group = [jnp.where(k == n, a, b) for a, b in zip(batches[n], group)]
-        return group
+                pos_copy(src, k).start()
 
     @pl.loop(0, 1)
     def _(k):
-        gather(one_of(k))
-
-
-    @pl.loop(1, chips)
-    def _(off):
-        src = lax.rem(chip + off, chips)
-        wait_recv(negbuf.at[mine, src], neg_s.at[src], neg_r.at[src], item=src * 2 + core)
-        wait_recv(nidbuf.at[mine, src], nid_s.at[src], nid_r.at[src], item=src * 2 + core)
+        gather(k)
+
+
+    wait_all(negbuf.at[mine, pl.ds(0, chips - 1)], recv=neg_r)
+    wait_all(nidbuf.at[mine, pl.ds(0, chips - 1)], recv=nid_r)
 
     half = chips // 2
 
     def piece_part(d, h):
         return negbuf.at[d * 2 + core, pl.ds(h * half, half)], nidbuf.at[d * 2 + core, pl.ds(h * half, half)]
 
-    def y_copies(d, h, way, dest):
+    def y_copies(d, h, dest):
         rows_part, ids_part = piece_part(d, h)
         return (
-            copy(rows_part, rows_part, pc_s.at[way, h], pc_r.at[d, h], dp=dest),
-            copy(ids_part, ids_part, pi_s.at[way, h], pi_r.at[d, h], dp=dest),
+            copy(rows_part, rows_part, pc_s, pc_r.at[d, h], dp=dest),
+            copy(ids_part, ids_part, pi_s, pi_r.at[d, h], dp=dest),
         )
 
     def y_wait(d, h, dest):
-        for c in y_copies(d, h, 0, dest):
+        for c in y_copies(d, h, dest):
             c.wait_recv()
 
     def sib_copies(d, side):
         piece = d * 2 + side
         return (
-            copy(negbuf.at[piece], negbuf.at[piece], sn_s.at[d], sn_r.at[d], item=sibling),
-            copy(nidbuf.at[piece], nidbuf.at[piece], si_s.at[d], si_r.at[d], item=sibling),
+            copy(negbuf.at[piece], negbuf.at[piece], sn_s, sn_r.at[d], item=sibling),
+            copy(nidbuf.at[piece], nidbuf.at[piece], si_s, si_r.at[d], item=sibling),
         )
 
     def to_sibling(d):
@@ -250,19 +262,19 @@
         for c in sib_copies(d, 1 - core):
             c.wait_recv()
 
-    def send_y(d, h, way, dest):
-        for c in y_copies(d, h, way, dest):
+    def send_y(d, h, dest):
+        for c in y_copies(d, h, dest):
             c.start()
 
-    send_y(y, 0, 0, up)
-    send_y(y, 1, 1, down)
-    send_y(y, 1, 0, up)
-    send_y(y, 0, 1, down)
+    send_y(y, 0, up)
+    send_y(y, 1, down)
+    send_y(y, 1, up)
+    send_y(y, 0, down)
     to_sibling(y)
 
     @pl.loop(1, len(batches))
     def _(k):
-        gather(one_of(k))
+        gather(k)
 
     returned[me] = found[me]
 
@@ -293,9 +305,9 @@
         pass1(y * 2 + side)
 
     y_wait(down, 0, down)
-    send_y(down, 0, 2, up)
+    send_y(down, 0, up)
     y_wait(up, 1, up)
-    send_y(up, 1, 2, down)
+    send_y(up, 1, down)
     y_wait(down, 1, down)
     to_sibling(down)
     y_wait(up, 0, up)
@@ -329,12 +341,7 @@
     @pl.loop(0, len(batches))
     def _(k):
         group = one_of(k)
-        for src in group:
-
-            @pl.when(src != me)
-            def _():
-                wait_recv(returned.at[src], pos_s.at[src], pos_r.at[src], item=src)
-
+        wait_batch(k, returned, pos_r)
         pick = (place_c == slots_of(group)).astype(BF)
         pos_f[...] += dot(pick, jnp.concatenate([returned[src] for src in group], axis=0))
 
@@ -349,8 +356,8 @@
 
     g_bf[...] = (INV_TEMP * coef * q_hat).astype(BF)
 
-    def g_copy(peer):
-        return copy(outbox.at[peer], inbox.at[me], g_s.at[peer], g_r.at[me], item=peer)
+    def g_copy(peer, k):
+        return copy(outbox.at[peer], inbox.at[me], g_s, g_r.at[k], item=peer)
 
     @pl.loop(0, len(batches))
     def _(k):
@@ -362,7 +369,7 @@
 
             @pl.when(src != me)
             def _():
-                g_copy(src).start()
+                g_copy(src, k).start()
 
     inbox[me] = outbox[me]
 
@@ -385,58 +392,107 @@
 
     to_sib.wait_recv()
 
-    @pl.loop(0, chips)
+    side = math.isqrt(chips)
+    nz, nx = (side, side) if side * side == chips else (1, chips)
+    my_z, my_x = chip // nx, lax.rem(chip, nx)
+    hn = n_dp * neg // 2
+
+    @pl.loop(0, nz)
     def _(z):
-        red_out[z] = (part[core, z].astype(F32) + sib_in[z].astype(F32)).astype(BF)
-
-    def red_copy(peer_chip):
-        return copy(red_out.at[peer_chip], red_in.at[chip], red_s.at[peer_chip], red_r.at[chip], item=peer_chip * 2 + core)
-
-    @pl.loop(1, chips)
-    def _(off):
-        red_copy(lax.rem(chip + off, chips)).start()
-
-    for k, group in enumerate(batches):
-        for src in group:
-
-            @pl.when(src != me)
-            def _():
-                wait_recv(inbox.at[src], g_s.at[src], g_r.at[src], item=src)
-
+        @pl.loop(0, nx)
+        def _(x):
+            at = z * nx + x
+            both = (part[core, at].astype(F32) + sib_in[at].astype(F32)).astype(BF)
+            by_x[x, z] = both[:hn]
+            by_z[z, x] = both[hn:]
+
+    def at_x(x):
+        return (my_z * nx + x) * 2 + core
+
+    def at_z(z):
+        return (z * nx + my_x) * 2 + core
+
+    def first_x(x):
+        return copy(by_x.at[x], in_x.at[my_x], hop_s.at[0], hop_r.at[0], item=at_x(x))
+
+    def first_z(z):
+        return copy(by_z.at[z], in_z.at[my_z], hop_s.at[1], hop_r.at[1], item=at_z(z))
+
+    def second_z(z):
+        return copy(mid_z.at[z], end_z.at[my_z], hop_s.at[2], hop_r.at[2], item=at_z(z))
+
+    def second_x(x):
+        return copy(mid_x.at[x], end_x.at[my_x], hop_s.at[3], hop_r.at[3], item=at_x(x))
+
+    def start_others(mine_at, count, make):
+        @pl.loop(1, count)
+        def _(off):
+            make(lax.rem(mine_at + off, count)).start()
+
+    def wait_others(buffer, count, **sem):
+        if count > 1:
+            wait_all(buffer.at[pl.ds(0, count - 1)], **sem)
+
+    start_others(my_x, nx, first_x)
+    start_others(my_z, nz, first_z)
+    in_x[my_x] = by_x[my_x]
+    in_z[my_z] = by_z[my_z]
+
+    def add_to_dense(group, d, fresh):
         ids = jnp.concatenate([req_in[src][:, :cap] for src in group], axis=1)
         came = jnp.concatenate([inbox[src] for src in group], axis=0)
+        at = pl.ds(pl.multiple_of(d * quarter, quarter), quarter)
+        new = dot(pick_rows(ids, (d * quarter).astype(F32), quarter), came)
+        if fresh:
+            dense_f[at, :] = new
+        else:
+            dense_f[at, :] += new
+
+    def wait_inbox(k):
+        wait_all(inbox.at[pl.ds(0, batch - 1 if k == own_batch else batch)], recv=g_r.at[k])
+
+    head, tail = batches[:-2], batches[-2:]
+    for k, group in enumerate(head):
+        wait_inbox(k)
 
         @pl.loop(0, n_dp)
         def _(d):
-            at = pl.ds(pl.multiple_of(d * quarter, quarter), quarter)
-            new = dot(pick_rows(ids, (d * quarter).astype(F32), quarter), came)
-            if k == 0:
-                dense_f[at, :] = new
-            else:
-                dense_f[at, :] += new
+            add_to_dense(group, d, k == 0)
+
+    for k in range(len(head), len(batches)):
+        wait_inbox(k)
+
+    def finish(d):
+        @pl.loop(0, 1)
+        def _(_):
+            add_to_dense([src for group in tail for src in group], d, not head)
 
     def rs_copies():
         return (
-            copy(rs_out.at[0, 0], relay_in.at[0], rs_s.at[0, 0], relay_r.at[0], dp=up),
-            copy(rs_out.at[0, 1], relay_in.at[1], rs_s.at[0, 1], relay_r.at[1], dp=down),
-            copy(rs_out.at[1, 0], rs_in.at[0, 0], rs_s.at[1, 0], rs_r.at[0, 0], dp=up),
-            copy(rs_out.at[1, 1], rs_in.at[0, 1], rs_s.at[1, 1], rs_r.at[0, 1], dp=up),
-            copy(rs_out.at[2, 0], rs_in.at[1, 0], rs_s.at[2, 0], rs_r.at[1, 0], dp=down),
-            copy(rs_out.at[2, 1], rs_in.at[1, 1], rs_s.at[2, 1], rs_r.at[1, 1], dp=down),
+            copy(rs_out.at[0, 0], relay_in.at[0], rs_s, relay_r.at[0], dp=up),
+            copy(rs_out.at[0, 1], relay_in.at[1], rs_s, relay_r.at[1], dp=down),
+            copy(rs_out.at[1, 0], rs_in.at[0, 0], rs_s, rs_r.at[0, 0], dp=up),
+            copy(rs_out.at[1, 1], rs_in.at[0, 1], rs_s, rs_r.at[0, 1], dp=up),
+            copy(rs_out.at[2, 0], rs_in.at[1, 0], rs_s, rs_r.at[1, 0], dp=down),
+            copy(rs_out.at[2, 1], rs_in.at[1, 1], rs_s, rs_r.at[1, 1], dp=down),
         )
 
     def dense_part(d, h):
         return dense_f[pl.ds(pl.multiple_of(d * quarter + h * hq, hq), hq), :]
 
     far0, far1, up0, up1, down0, down1 = rs_copies()
+    finish(far)
     rs_out[0, 0] = dense_part(far, 0).astype(BF)
     far0.start()
     rs_out[0, 1] = dense_part(far, 1).astype(BF)
     far1.start()
+    finish(up)
     rs_out[1, 1] = dense_part(up, 1).astype(BF)
     up1.start()
+    finish(down)
     rs_out[2, 0] = dense_part(down, 0).astype(BF)
     down0.start()
+    finish(y)
     far0.wait_recv()
     rs_out[1, 0] = (dense_part(up, 0) + relay_in[0].astype(F32)).astype(BF)
     up0.start()
@@ -444,6 +500,22 @@
     rs_out[2, 1] = (dense_part(down, 1) + relay_in[1].astype(F32)).astype(BF)
     down1.start()
 
+    wait_others(in_x, nx, recv=hop_r.at[0])
+    wait_others(in_z, nz, recv=hop_r.at[1])
+
+    def added(buffer):
+        total = buffer[0].astype(F32)
+        for n in range(1, buffer.shape[0]):
+            total += buffer[n].astype(F32)
+        return total.astype(BF)
+
+    mid_z[...] = added(in_x)
+    mid_x[...] = added(in_z)
+    start_others(my_z, nz, second_z)
+    start_others(my_x, nx, second_x)
+    end_z[my_z] = mid_z[my_z]
+    end_x[my_x] = mid_x[my_x]
+
     ut[...] = jnp.zeros_like(ut)
 
     @pl.loop(0, 2 * n_dp)
@@ -455,48 +527,37 @@
     g_q = INV_TEMP * (coef * pos_f[...] + jnp.transpose(ut[...]) * inv_tot)
     grad_ref[...] = ((g_q - acc[...] * jnp.sum(acc[...] * g_q, axis=1, keepdims=True)) / q_norm).astype(BF)
 
-    @pl.loop(1, n_item)
-    def _(off):
-        peer = lax.rem(me + off, n_item)
-        req_copy(peer).wait_send()
-        pos_copy(peer).wait_send()
-        g_copy(peer).wait_send()
-
-    @pl.loop(1, chips)
-    def _(off):
-        peer = lax.rem(chip + off, chips)
-        for c in plane_copies(peer):
-            c.wait_send()
-        red_copy(peer).wait_send()
-
-    @pl.loop(0, n_dp)
-    def _(d):
-        for c in sib_copies(d, core):
-            c.wait_send()
-
-    for h in range(2):
-        for c in (*y_copies(y, h, 0, up), *y_copies(y, h, 1, down)):
-            c.wait_send()
-    for c in (*y_copies(down, 0, 2, up), *y_copies(up, 1, 2, down)):
-        c.wait_send()
-
-    total = red_out[chip].astype(F32)
-
-    def add_red(off, total):
-        src = lax.rem(chip + off, chips)
-        wait_recv(red_in.at[src], red_s.at[src], red_r.at[src], item=src * 2 + core)
-        return total + red_in[src].astype(F32)
-
-    total = lax.fori_loop(1, chips, add_red, total)
-    y_in[y] = total.astype(BF)
+    wait_all(req_out.at[pl.ds(0, n_item - 1)], send=req_s)
+    wait_all(found.at[pl.ds(0, n_item - 1)], send=pos_s)
+    wait_all(outbox.at[pl.ds(0, n_item - 1)], send=g_s)
+    wait_all(negbuf.at[mine, pl.ds(0, chips - 1)], send=neg_s)
+    wait_all(nidbuf.at[mine, pl.ds(0, chips - 1)], send=nid_s)
+    wait_all(negbuf.at[pl.ds(0, 3)], send=pc_s)
+    wait_all(nidbuf.at[pl.ds(0, 3)], send=pi_s)
+    wait_all(negbuf.at[pl.ds(0, n_dp)], send=sn_s)
+    wait_all(nidbuf.at[pl.ds(0, n_dp)], send=si_s)
+    to_sib.wait_send()
+    wait_others(by_x, nx, send=hop_s.at[0])
+    wait_others(by_z, nz, send=hop_s.at[1])
+
+    wait_others(end_z, nz, recv=hop_r.at[2])
+    wait_others(end_x, nx, recv=hop_r.at[3])
+    sums = jnp.concatenate([added(end_z), added(end_x)], axis=0)
+    for d in range(n_dp):
+        y_out[d] = sums[d * neg : (d + 1) * neg]
+    y_in[y] = y_out[y]
+
+    def part_copy(dest):
+        return copy(y_out.at[dest], y_in.at[y], y_s.at[0], y_r.at[0], dp=dest)
 
     def sum_copy(dest):
-        return copy(y_in.at[y], y_in.at[y], y_s.at[dest], y_r.at[y], dp=dest)
-
-    @pl.loop(1, n_dp)
-    def _(off):
-        sum_copy(lax.rem(y + off, n_dp)).start()
-
+        return copy(y_sum.at[y], y_sum.at[y], y_s.at[1], y_r.at[1], dp=dest)
+
+    start_others(y, n_dp, part_copy)
+
+    wait_others(y_in, n_dp, recv=y_r.at[0])
+    y_sum[y] = added(y_in)
+    start_others(y, n_dp, sum_copy)
     up1.wait_recv()
     up0.wait_recv()
     down0.wait_recv()
@@ -504,29 +565,22 @@
     for h in range(2):
         ag[y, h] = (dense_part(y, h) + rs_in[0, h].astype(F32) + rs_in[1, h].astype(F32)).astype(BF)
 
-    def ag_copy(slot, h, way, dest):
-        return copy(ag.at[slot, h], ag.at[slot, h], ag_s.at[way, h], ag_r.at[slot, h], dp=dest)
-
-    for h in range(2):
-        ag_copy(y, h, 0, up).start()
-        ag_copy(y, h, 1, down).start()
-    @pl.loop(1, n_dp)
-    def _(off):
-        src = lax.rem(y + off, n_dp)
-        wait_recv(y_in.at[src], y_s.at[src], y_r.at[src], dp=src)
-
-    sums = y_in[0].astype(F32)
-    for d in range(1, n_dp):
-        sums += y_in[d].astype(F32)
-    sums_high = sums.astype(BF)
-    sums_low = (sums - sums_high.astype(F32)).astype(BF)
+    def ag_copy(slot, h, dest):
+        return copy(ag.at[slot, h], ag.at[slot, h], ag_s, ag_r.at[slot, h], dp=dest)
+
+    ag_copy(y, 0, up).start()
+    ag_copy(y, 1, down).start()
+    ag_copy(y, 1, up).start()
+    ag_copy(y, 0, down).start()
+    wait_others(y_sum, n_dp, recv=y_r.at[1])
+    neg_sums = y_sum[...].reshape(n_dp * neg, width)
     neg_ids = jnp.concatenate([nidbuf[d * 2 + core, chip][:, :neg] for d in range(n_dp)], axis=1)
 
     def step(d, h):
         first = d * quarter + h * hq
         at = pl.ds(pl.multiple_of(first, hq), hq)
         pick = (neg_ids == iota((hq, n_dp * neg), 0) + first.astype(F32)).astype(BF)
-        g = ag[d, h].astype(F32) + dot(pick, sums_high) + dot(pick, sums_low)
+        g = ag[d, h].astype(F32) + dot(pick, neg_sums)
         t = table_ref[at, :]
         norm = jnp.sqrt(jnp.sum(t * t, axis=1, keepdims=True) + EPSILON)
         unit = t / norm
@@ -543,34 +597,36 @@
 
     step_both(y)
 
-    wait_recv(ag.at[down, 0], ag_s.at[0, 0], ag_r.at[down, 0], dp=down)
-    ag_copy(down, 0, 2, up).start()
-    wait_recv(ag.at[up, 1], ag_s.at[0, 1], ag_r.at[up, 1], dp=up)
-    ag_copy(up, 1, 2, down).start()
-
-    wait_recv(ag.at[down, 1], ag_s.at[0, 1], ag_r.at[down, 1], dp=down)
-    wait_recv(ag.at[up, 0], ag_s.at[0, 0], ag_r.at[up, 0], dp=up)
+    wait_recv(ag.at[down, 0], ag_s, ag_r.at[down, 0], dp=down)
+    ag_copy(down, 0, up).start()
+    wait_recv(ag.at[up, 1], ag_s, ag_r.at[up, 1], dp=up)
+    ag_copy(up, 1, down).start()
+
+    wait_recv(ag.at[down, 1], ag_s, ag_r.at[down, 1], dp=down)
+    wait_recv(ag.at[up, 0], ag_s, ag_r.at[up, 0], dp=up)
 
     @pl.loop(0, 2)
     def _(k):
         step_both(lax.rem(y + 1 + 2 * k, n_dp))
 
-    wait_recv(ag.at[far, 0], ag_s.at[0, 0], ag_r.at[far, 0], dp=down)
-    wait_recv(ag.at[far, 1], ag_s.at[0, 1], ag_r.at[far, 1], dp=up)
+    wait_recv(ag.at[far, 0], ag_s, ag_r.at[far, 0], dp=down)
+    wait_recv(ag.at[far, 1], ag_s, ag_r.at[far, 1], dp=up)
     step_both(far)
 
-    @pl.loop(1, n_dp)
-    def _(off):
-        sum_copy(lax.rem(y + off, n_dp)).wait_send()
-
-    to_sib.wait_send()
-    for c in rs_copies():
-        c.wait_send()
-    for h in range(2):
-        ag_copy(y, h, 0, up).wait_send()
-        ag_copy(y, h, 1, down).wait_send()
-    ag_copy(down, 0, 2, up).wait_send()
-    ag_copy(up, 1, 2, down).wait_send()
+    wait_others(mid_z, nz, send=hop_s.at[2])
+    wait_others(mid_x, nx, send=hop_s.at[3])
+    wait_others(y_out, n_dp, send=y_s.at[0])
+    wait_others(y_sum, n_dp, send=y_s.at[1])
+    wait_all(rs_out, send=rs_s)
+    wait_all(ag.at[pl.ds(0, 3)], send=ag_s)
+
+
+def write_kernel(*refs):
+    copies = [pltpu.make_async_copy(refs[k], refs[4 + k], refs[8].at[k]) for k in range(4)]
+    for c in copies:
+        c.start()
+    for c in copies:
+        c.wait()
 
 
 def on_device(n_dp, n_item, queries, item_table, adagrad_state, pos_owner, pos_row, neg_rows):
@@ -583,6 +639,10 @@
     vmem, hbm = pl.BlockSpec(memory_space=pltpu.VMEM), pl.BlockSpec(memory_space=pl.ANY)
     dma = pltpu.SemaphoreType.DMA
     n_neg = 2 * n_dp * chips * neg
+    n_batches = n_item // min(8, n_item)
+    side = math.isqrt(chips)
+    nz, nx = (side, side) if side * side == chips else (1, chips)
+    hn = n_dp * neg // 2
     flops = 2 * width * (3 * n_neg * ex + 3 * n_item * cap * (rows + ex))
     grad, loss, new_table, new_state = pl.pallas_call(
         functools.partial(main_kernel, n_dp, n_item),
@@ -614,29 +674,37 @@
             pltpu.VMEM((2 * n_dp, chips, neg, ex), BF),
             pltpu.VMEM((2, chips, n_dp * neg, width), BF),
             pltpu.VMEM((chips, n_dp * neg, width), BF),
-            pltpu.VMEM((chips, n_dp * neg, width), BF),
-            pltpu.VMEM((chips, n_dp * neg, width), BF),
-            pltpu.VMEM((n_dp, n_dp * neg, width), BF),
+            pltpu.VMEM((nx, nz, hn, width), BF),
+            pltpu.VMEM((nz, nx, hn, width), BF),
+            pltpu.VMEM((nx, nz, hn, width), BF),
+            pltpu.VMEM((nz, nx, hn, width), BF),
+            pltpu.VMEM((nx, hn, width), BF),
+            pltpu.VMEM((nz, hn, width), BF),
+            pltpu.VMEM((nx, hn, width), BF),
+            pltpu.VMEM((nz, hn, width), BF),
+            pltpu.VMEM((n_dp, neg, width), BF),
+            pltpu.VMEM((n_dp, neg, width), BF),
+            pltpu.VMEM((n_dp, neg, width), BF),
             pltpu.VMEM((rows, width), F32),
             pltpu.VMEM((3, 2, quarter // 2, width), BF),
             pltpu.VMEM((2, quarter // 2, width), BF),
             pltpu.VMEM((2, 2, quarter // 2, width), BF),
             pltpu.VMEM((n_dp, 2, quarter // 2, width), BF),
-            dma((n_item,)), dma((n_item,)),
-            dma((chips,)), dma((chips,)),
-            dma((chips,)), dma((chips,)),
-            dma((3, 2)), dma((n_dp, 2)),
-            dma((3, 2)), dma((n_dp, 2)),
-            dma((n_dp,)), dma((n_dp,)),
-            dma((n_dp,)), dma((n_dp,)),
-            dma((n_item,)), dma((n_item,)),
-            dma((n_item,)), dma((n_item,)),
             dma, dma,
-            dma((chips,)), dma((chips,)),
-            dma((n_dp,)), dma((n_dp,)),
-            dma((3, 2)), dma((2,)), dma((2, 2)),
-            dma((3, 2)), dma((n_dp, 2)),
-            dma((2 * n_dp,)),
+            dma, dma,
+            dma, dma,
+            dma, dma((n_dp, 2)),
+            dma, dma((n_dp, 2)),
+            dma, dma((n_dp,)),
+            dma, dma((n_dp,)),
+            dma, dma((n_batches,)),
+            dma, dma((n_batches,)),
+            dma, dma,
+            dma((4,)), dma((4,)),
+            dma((2,)), dma((2,)),
+            dma, dma((2,)), dma((2, 2)),
+            dma, dma((n_dp, 2)),
+            dma,
         ],
         compiler_params=pltpu.CompilerParams(collective_id=0, has_side_effects=True, vmem_limit_bytes=56 * 2**20),
         cost_estimate=pl.CostEstimate(flops=flops, bytes_accessed=12 * 2**20, transcendentals=n_neg * ex),
@@ -645,6 +713,17 @@
         neg_rows, queries, item_table, adagrad_state.reshape(1, rows), pos_owner.reshape(1, ex), pos_row.reshape(1, ex),
         neg_rows.reshape(1, neg),
     )
+
+    made = [pltpu.with_memory_space_constraint(a, pltpu.VMEM) for a in (grad, loss, new_table, new_state)]
+    grad, loss, new_table, new_state = pl.pallas_call(
+        write_kernel,
+        out_shape=[jax.ShapeDtypeStruct(a.shape, a.dtype) for a in made],
+        in_specs=[vmem] * 4,
+        out_specs=[hbm] * 4,
+        scratch_shapes=[dma((4,))],
+        compiler_params=pltpu.CompilerParams(vmem_limit_bytes=2**20),
+        name="write_results",
+    )(*made)
     return grad, loss.reshape(ex), new_table, new_state.reshape(rows)
 
 

time: 120 us -> 109 us (0.908)
  Pallas kernels: 114 us -> 108 us
  local copies, waits for them, and re-layouts: 4.01 us -> 0 us
    pallas_call x1, Pallas kernels: 114 us -> 105 us  [on_device(): pl.pallas_call(functools.partial(main_kernel, n_dp, n_item), out_shape=(p...]
    unnamed x4 -> x0, local copies, waits for them, and re-layouts: 4.01 us -> none
    pallas_call x0 -> x1, Pallas kernels: none -> 2.23 us  [on_device(): pl.pallas_call(write_kernel, out_shape=[jax.ShapeDtypeStruct(a.shape, a.d...]
where the time goes in v4:
time: 109 us; the launch traced here: 108 us
  Pallas kernels  108 us (99%)
    pallas_call x1, Pallas kernels, on_device(): pl.pallas_call(functools.partial(main_kernel, n_dp, n_item), out_shape=(p...  105 us
    pallas_call x1, Pallas kernels, on_device(): pl.pallas_call(write_kernel, out_shape=[jax.ShapeDtypeStruct(a.shape, a.d...  2.23 us

profile of v4, /device:TPU:1, one launch (start us, length us, event | category | flops | bytes accessed | tf_op | source)
XLA Modules:
  0.0 108.3 jit_solution(7682778257675051160)
XLA Ops:
  0.6 105.3 %training_step.1 = (bf16[1024,256]{1,0:T(8,128)(2,1)S(1)}, f32[1,1024]{1,0:T(1,128)S(1)}, f32[4096,256]{1,0:T(8,128)S(1)}, f32[1,4096]{1,0:T(1,128)S(1)}) custom-call(s32[48]{0:T(128)} %neg_s_ref.1, bf16[1024,256]{1,0:T(8,128)(2,1)} %q_ref.1, f32[4096,256]{1,0:T(8,128)} %table_hbm.1, f32[1,4096]{1,0:T(1,128)} %bitcast.6, s32[1,1024]{1,0:T(1,128)} %bitcast.8, ...), custom_call_target="tpu_custom_call" | custom-call | flops 33822867456 | bytes 12582912 | tf_op jit(solution)/shard_map/training_step/pallas_call | solution.py:647
  105.9 2.2 %write_results.1 = (bf16[1024,256]{1,0:T(8,128)(2,1)}, f32[1,1024]{1,0:T(1,128)}, f32[4096,256]{1,0:T(8,128)}, f32[1,4096]{1,0:T(1,128)}) custom-call(bf16[1024,256]{1,0:T(8,128)(2,1)S(1)} %get-tuple-element.12.refs_0_, f32[1,1024]{1,0:T(1,128)S(1)} %get-tuple-element.13.refs_1_, f32[4096,256]{1,0:T(8,128)S(1)} %get-tuple-element.14.refs_2_, ...), custom_call_target="tpu_custom_call" | custom-call | tf_op jit(solution)/shard_map/write_results/pallas_call | solution.py:718

commit v5 on v4

--- a/solution.py
+++ b/solution.py
@@ -60,12 +60,12 @@
 
 def main_kernel(
     n_dp, n_item,
-    neg_s_ref, q_ref, table_hbm, state_ref, owner_ref, row_ref, neg_ref,
+    neg_s_ref, q_hbm, table_hbm, state_ref, owner_ref, row_ref, neg_ref,
     grad_ref, loss_ref, table_ref, state_out,
-    neg_f, tsend, qt, req_out, req_in, negbuf, nidbuf, found, returned, outbox, inbox, acc, pos_f, g_bf, ut, tot, et, part, sib_in, by_x, by_z, in_x, in_z, mid_x, mid_z, end_x, end_z, y_out, y_in, y_sum,
+    q_ref, neg_f, tsend, qt, req_out, req_in, negbuf, nidbuf, found, returned, outbox, inbox, acc, pos_f, g_bf, ut, tot, et, part, sib_in, by_x, by_z, in_x, in_z, mid_x, mid_z, end_x, end_z, y_out, y_in, y_sum,
     dense_f, rs_out, relay_in, rs_in, ag,
     req_s, req_r, neg_s, neg_r, nid_s, nid_r, pc_s, pc_r, pi_s, pi_r, sn_s, sn_r, si_s, si_r, pos_s, pos_r, g_s, g_r, sib_s, sib_r, hop_s, hop_r, y_s, y_r,
-    rs_s, relay_r, rs_r, ag_s, ag_r, load_s,
+    rs_s, relay_r, rs_r, ag_s, ag_r, load_s, load_q,
 ):
     ex, width = q_ref.shape
     rows = table_ref.shape[0]
@@ -91,6 +91,9 @@
     @pl.loop(0, 2 * n_dp)
     def _(k):
         load(k).start()
+
+    load_queries = pltpu.make_async_copy(q_hbm, q_ref, load_q)
+    load_queries.start()
 
     def wait_all(part, send=None, recv=None):
         c = copy(part, part, recv if send is None else send, send if recv is None else recv, item=sibling)
@@ -172,6 +175,7 @@
         t = table_ref[at, :]
         tsend[at, :] = (t / jnp.sqrt(jnp.sum(t * t, axis=1, keepdims=True) + EPSILON)).astype(BF)
 
+    load_queries.wait()
     q = q_ref[...].astype(F32)
     q_norm = jnp.sqrt(jnp.sum(q * q, axis=1, keepdims=True) + EPSILON)
     acc[...] = q / q_norm
@@ -247,19 +251,19 @@
         for c in y_copies(d, h, dest):
             c.wait_recv()
 
-    def sib_copies(d, side):
-        piece = d * 2 + side
+    def sib_copies(d, side, h):
+        piece, at = d * 2 + side, pl.ds(h * half, half)
         return (
-            copy(negbuf.at[piece], negbuf.at[piece], sn_s, sn_r.at[d], item=sibling),
-            copy(nidbuf.at[piece], nidbuf.at[piece], si_s, si_r.at[d], item=sibling),
+            copy(negbuf.at[piece, at], negbuf.at[piece, at], sn_s, sn_r.at[d, h], item=sibling),
+            copy(nidbuf.at[piece, at], nidbuf.at[piece, at], si_s, si_r.at[d, h], item=sibling),
         )
 
-    def to_sibling(d):
-        for c in sib_copies(d, core):
+    def to_sibling(d, h):
+        for c in sib_copies(d, core, h):
             c.start()
 
-    def from_sibling(d):
-        for c in sib_copies(d, 1 - core):
+    def from_sibling(d, h):
+        for c in sib_copies(d, 1 - core, h):
             c.wait_recv()
 
     def send_y(d, h, dest):
@@ -270,7 +274,8 @@
     send_y(y, 1, down)
     send_y(y, 1, up)
     send_y(y, 0, down)
-    to_sibling(y)
+    to_sibling(y, 0)
+    to_sibling(y, 1)
 
     @pl.loop(1, len(batches))
     def _(k):
@@ -280,56 +285,68 @@
 
     tot[...] = jnp.zeros_like(tot)
 
-    def pass1(piece):
-        @pl.loop(0, chips // half)
-        def _(h):
-            first = h * half
-            block = negbuf[piece, pl.ds(first, half)].reshape(half * neg, width)
-            ids = jnp.concatenate(
-                [
-                    row_to_col(nidbuf[piece, first + z])[:neg]
-                    + (((first + z) * 2 + lax.rem(piece, 2)) * rows).astype(F32)
-                    for z in range(half)
-                ],
-                axis=0,
-            )
-            e = jnp.where(ids != gid_r, jnp.exp2(dot(block, qt[...]) * (INV_TEMP * LOG2E)), 0.0)
-            tot[...] += jnp.sum(e.reshape(half * neg // 8, 8, ex), axis=0)
-            eb = e.astype(BF)
-            et[piece, pl.ds(first, half)] = eb.reshape(half, neg, ex)
-
-    from_sibling(y)
-
-    @pl.loop(0, 2)
-    def _(side):
-        pass1(y * 2 + side)
+    def pass1(piece, h):
+        first = h * half
+        block = negbuf[piece, pl.ds(first, half)].reshape(half * neg, width)
+        ids = jnp.concatenate(
+            [
+                row_to_col(nidbuf[piece, first + z])[:neg]
+                + (((first + z) * 2 + lax.rem(piece, 2)) * rows).astype(F32)
+                for z in range(half)
+            ],
+            axis=0,
+        )
+        e = jnp.where(ids != gid_r, jnp.exp2(dot(block, qt[...]) * (INV_TEMP * LOG2E)), 0.0)
+        tot[...] += jnp.sum(e.reshape(half * neg // 8, 8, ex), axis=0)
+        eb = e.astype(BF)
+        et[piece, pl.ds(first, half)] = eb.reshape(half, neg, ex)
+
+    from_sibling(y, 0)
+    from_sibling(y, 1)
+
+    @pl.loop(0, 4)
+    def _(k):
+        pass1(y * 2 + k // 2, lax.rem(k, 2))
+
+    def near(side, first):
+        @pl.loop(0, 2)
+        def _(k):
+            pass1(lax.rem(y + 3 - 2 * k, n_dp) * 2 + side, first + k - 2 * first * k)
 
     y_wait(down, 0, down)
     send_y(down, 0, up)
+    to_sibling(down, 0)
     y_wait(up, 1, up)
     send_y(up, 1, down)
+    to_sibling(up, 1)
+    near(core, 0)
+    from_sibling(down, 0)
+    from_sibling(up, 1)
+    near(1 - core, 0)
+
     y_wait(down, 1, down)
-    to_sibling(down)
+    to_sibling(down, 1)
     y_wait(up, 0, up)
-    to_sibling(up)
-
-    @pl.loop(0, 2)
-    def _(k):
-        pass1(lax.rem(y + 1 + 2 * k, n_dp) * 2 + core)
-
-    from_sibling(down)
-    from_sibling(up)
-
-    @pl.loop(0, 2)
-    def _(k):
-        pass1(lax.rem(y + 1 + 2 * k, n_dp) * 2 + 1 - core)
+    to_sibling(up, 0)
+    near(core, 1)
+    from_sibling(down, 1)
+    from_sibling(up, 0)
+    near(1 - core, 1)
 
     y_wait(far, 0, down)
+    to_sibling(far, 0)
     y_wait(far, 1, up)
-    to_sibling(far)
-    pass1(far * 2 + core)
-    from_sibling(far)
-    pass1(far * 2 + 1 - core)
+    to_sibling(far, 1)
+
+    def pass1_far(side):
+        @pl.loop(0, 2)
+        def _(h):
+            pass1(far * 2 + side, h)
+
+    pass1_far(core)
+    from_sibling(far, 0)
+    from_sibling(far, 1)
+    pass1_far(1 - core)
 
     place_c = row_to_col(place_r)
     pos_f[...] = jnp.zeros_like(pos_f)
@@ -338,13 +355,15 @@
         first = lax.broadcasted_iota(jnp.int32, (1, cap), 1)
         return jnp.concatenate([first + src * cap for src in group], axis=1).astype(F32)
 
-    @pl.loop(0, len(batches))
-    def _(k):
-        group = one_of(k)
-        wait_batch(k, returned, pos_r)
-        pick = (place_c == slots_of(group)).astype(BF)
-        pos_f[...] += dot(pick, jnp.concatenate([returned[src] for src in group], axis=0))
-
+    def place(first, end):
+        @pl.loop(first, end)
+        def _(k):
+            group = one_of(k)
+            wait_batch(k, returned, pos_r)
+            pick = (place_c == slots_of(group)).astype(BF)
+            pos_f[...] += dot(pick, jnp.concatenate([returned[src] for src in group], axis=0))
+
+    place(0, len(batches))
     q_hat = acc[...]
     pos_e = pos_f[...]
     s_pos = INV_TEMP * jnp.sum(q_hat.astype(BF).astype(F32) * pos_e, axis=1, keepdims=True)
@@ -462,11 +481,6 @@
     for k in range(len(head), len(batches)):
         wait_inbox(k)
 
-    def finish(d):
-        @pl.loop(0, 1)
-        def _(_):
-            add_to_dense([src for group in tail for src in group], d, not head)
-
     def rs_copies():
         return (
             copy(rs_out.at[0, 0], relay_in.at[0], rs_s, relay_r.at[0], dp=up),
@@ -481,18 +495,30 @@
         return dense_f[pl.ds(pl.multiple_of(d * quarter + h * hq, hq), hq), :]
 
     far0, far1, up0, up1, down0, down1 = rs_copies()
-    finish(far)
-    rs_out[0, 0] = dense_part(far, 0).astype(BF)
-    far0.start()
-    rs_out[0, 1] = dense_part(far, 1).astype(BF)
-    far1.start()
-    finish(up)
-    rs_out[1, 1] = dense_part(up, 1).astype(BF)
-    up1.start()
-    finish(down)
-    rs_out[2, 0] = dense_part(down, 0).astype(BF)
-    down0.start()
-    finish(y)
+    tail_group = [src for group in tail for src in group]
+
+    @pl.loop(0, n_dp)
+    def _(k):
+        step_k = jnp.where(k == 0, 2, jnp.where(k == 1, 1, jnp.where(k == 2, 3, 0)))
+        add_to_dense(tail_group, lax.rem(y + step_k, n_dp), not head)
+
+        @pl.when(k == 0)
+        def _():
+            rs_out[0, 0] = dense_part(far, 0).astype(BF)
+            far0.start()
+            rs_out[0, 1] = dense_part(far, 1).astype(BF)
+            far1.start()
+
+        @pl.when(k == 1)
+        def _():
+            rs_out[1, 1] = dense_part(up, 1).astype(BF)
+            up1.start()
+
+        @pl.when(k == 2)
+        def _():
+            rs_out[2, 0] = dense_part(down, 0).astype(BF)
+            down0.start()
+
     far0.wait_recv()
     rs_out[1, 0] = (dense_part(up, 0) + relay_in[0].astype(F32)).astype(BF)
     up0.start()
@@ -621,8 +647,12 @@
     wait_all(ag.at[pl.ds(0, 3)], send=ag_s)
 
 
-def write_kernel(*refs):
-    copies = [pltpu.make_async_copy(refs[k], refs[4 + k], refs[8].at[k]) for k in range(4)]
+def write_kernel(grad_v, loss_v, table_v, state_v, grad, loss, table, state, sems):
+    parts = sems.shape[0] - 3
+    rows = table.shape[0] // parts
+    pairs = [(table_v.at[pl.ds(k * rows, rows), :], table.at[pl.ds(k * rows, rows), :]) for k in range(parts)]
+    pairs += [(grad_v, grad), (state_v, state), (loss_v, loss)]
+    copies = [pltpu.make_async_copy(src, dst, sems.at[k]) for k, (src, dst) in enumerate(pairs)]
     for c in copies:
         c.start()
     for c in copies:
@@ -652,9 +682,10 @@
             pltpu.VMEM((rows, width), F32),
             pltpu.VMEM((1, rows), F32),
         ),
-        in_specs=[pl.BlockSpec(memory_space=pltpu.SMEM), vmem, hbm, vmem, vmem, vmem, vmem],
+        in_specs=[pl.BlockSpec(memory_space=pltpu.SMEM), hbm, hbm, vmem, vmem, vmem, vmem],
         out_specs=(vmem, vmem, vmem, vmem),
         scratch_shapes=[
+            pltpu.VMEM((ex, width), BF),
             pltpu.VMEM((neg, width), F32),
             pltpu.VMEM((rows, width), BF),
             pltpu.VMEM((width, ex), BF),
@@ -695,8 +726,8 @@
             dma, dma,
             dma, dma((n_dp, 2)),
             dma, dma((n_dp, 2)),
-            dma, dma((n_dp,)),
-            dma, dma((n_dp,)),
+            dma, dma((n_dp, 2)),
+            dma, dma((n_dp, 2)),
             dma, dma((n_batches,)),
             dma, dma((n_batches,)),
             dma, dma,
@@ -704,7 +735,7 @@
             dma((2,)), dma((2,)),
             dma, dma((2,)), dma((2, 2)),
             dma, dma((n_dp, 2)),
-            dma,
+            dma, dma,
         ],
         compiler_params=pltpu.CompilerParams(collective_id=0, has_side_effects=True, vmem_limit_bytes=56 * 2**20),
         cost_estimate=pl.CostEstimate(flops=flops, bytes_accessed=12 * 2**20, transcendentals=n_neg * ex),
@@ -720,7 +751,7 @@
         out_shape=[jax.ShapeDtypeStruct(a.shape, a.dtype) for a in made],
         in_specs=[vmem] * 4,
         out_specs=[hbm] * 4,
-        scratch_shapes=[dma((4,))],
+        scratch_shapes=[dma((11,))],
         compiler_params=pltpu.CompilerParams(vmem_limit_bytes=2**20),
         name="write_results",
     )(*made)

time: 109 us -> 108 us (level)
  no operation moved by 1% of the time
where the time goes in v5:
time: 108 us; the launch traced here: 107 us
  Pallas kernels  107 us (99%)
    pallas_call x1, Pallas kernels, on_device(): pl.pallas_call(functools.partial(main_kernel, n_dp, n_item), out_shape=(p...  104 us
    pallas_call x1, Pallas kernels, on_device(): pl.pallas_call(write_kernel, out_shape=[jax.ShapeDtypeStruct(a.shape, a.d...  2.28 us

profile of v5, /device:TPU:1, one launch (start us, length us, event | category | flops | bytes accessed | tf_op | source)
XLA Modules:
  0.0 107.4 jit_solution(1909992035471159526)
XLA Ops:
  0.6 104.3 %training_step.1 = (bf16[1024,256]{1,0:T(8,128)(2,1)S(1)}, f32[1,1024]{1,0:T(1,128)S(1)}, f32[4096,256]{1,0:T(8,128)S(1)}, f32[1,4096]{1,0:T(1,128)S(1)}) custom-call(s32[48]{0:T(128)} %neg_s_ref.1, bf16[1024,256]{1,0:T(8,128)(2,1)} %q_hbm.1, f32[4096,256]{1,0:T(8,128)} %table_hbm.1, f32[1,4096]{1,0:T(1,128)} %bitcast.6, s32[1,1024]{1,0:T(1,128)} %bitcast.8, ...), custom_call_target="tpu_custom_call" | custom-call | flops 33822867456 | bytes 12582912 | tf_op jit(solution)/shard_map/training_step/pallas_call | solution.py:677
  104.9 2.3 %write_results.1 = (bf16[1024,256]{1,0:T(8,128)(2,1)}, f32[1,1024]{1,0:T(1,128)}, f32[4096,256]{1,0:T(8,128)}, f32[1,4096]{1,0:T(1,128)}) custom-call(bf16[1024,256]{1,0:T(8,128)(2,1)S(1)} %get-tuple-element.12.grad_v, f32[1,1024]{1,0:T(1,128)S(1)} %get-tuple-element.13.loss_v, f32[4096,256]{1,0:T(8,128)S(1)} %get-tuple-element.14.table_v, ...), custom_call_target="tpu_custom_call" | custom-call | tf_op jit(solution)/shard_map/write_results/pallas_call | solution.py:749

commit v6 on v5

--- a/solution.py
+++ b/solution.py
@@ -373,10 +373,11 @@
     coef = jnp.exp(s_pos - lse) - 1.0
     inv_tot = jnp.exp(-lse)
 
+    fw = width // 2
     g_bf[...] = (INV_TEMP * coef * q_hat).astype(BF)
 
-    def g_copy(peer, k):
-        return copy(outbox.at[peer], inbox.at[me], g_s, g_r.at[k], item=peer)
+    def g_copy(f, peer, k):
+        return copy(outbox.at[f, peer], inbox.at[f, me], g_s.at[f], g_r.at[f, k], item=peer)
 
     @pl.loop(0, len(batches))
     def _(k):
@@ -384,13 +385,23 @@
         wanted = jnp.concatenate([iota((cap, 1), 0) + (src * cap).astype(F32) for src in group], axis=0)
         rows_out = dot((place_r == wanted).astype(BF), g_bf[...])
         for s, src in enumerate(group):
-            outbox[src] = rows_out[s * cap : (s + 1) * cap].astype(BF)
+            for f in range(2):
+                outbox[f, src] = rows_out[s * cap : (s + 1) * cap, f * fw : (f + 1) * fw].astype(BF)
 
             @pl.when(src != me)
             def _():
-                g_copy(src, k).start()
-
-    inbox[me] = outbox[me]
+                g_copy(0, src, k).start()
+
+    @pl.loop(0, len(batches))
+    def _(k):
+        for src in one_of(k):
+
+            @pl.when(src != me)
+            def _():
+                g_copy(1, src, k).start()
+
+    inbox[0, me] = outbox[0, me]
+    inbox[1, me] = outbox[1, me]
 
     q_scaled = (q_hat.astype(BF).astype(F32) * (INV_TEMP * inv_tot)).astype(BF)
 
@@ -457,74 +468,63 @@
     in_x[my_x] = by_x[my_x]
     in_z[my_z] = by_z[my_z]
 
-    def add_to_dense(group, d, fresh):
-        ids = jnp.concatenate([req_in[src][:, :cap] for src in group], axis=1)
-        came = jnp.concatenate([inbox[src] for src in group], axis=0)
-        at = pl.ds(pl.multiple_of(d * quarter, quarter), quarter)
-        new = dot(pick_rows(ids, (d * quarter).astype(F32), quarter), came)
-        if fresh:
-            dense_f[at, :] = new
-        else:
-            dense_f[at, :] += new
-
-    def wait_inbox(k):
-        wait_all(inbox.at[pl.ds(0, batch - 1 if k == own_batch else batch)], recv=g_r.at[k])
-
-    head, tail = batches[:-2], batches[-2:]
-    for k, group in enumerate(head):
-        wait_inbox(k)
-
+    def wait_inbox(f):
+        for k in range(len(batches)):
+            wait_all(inbox.at[f, pl.ds(0, batch - 1 if k == own_batch else batch)], recv=g_r.at[f, k])
+
+    def quarter_sum(f, d):
+        total = jnp.zeros((quarter, fw), F32)
+        for k in range(0, n_item, batch):
+            ids = jnp.concatenate([req_in[src][:, :cap] for src in range(k, k + batch)], axis=1)
+            came = inbox[f, k : k + batch].reshape(batch * cap, fw)
+            total += dot(pick_rows(ids, (d * quarter).astype(F32), quarter), came)
+        dense_f[f, pl.ds(pl.multiple_of(d * quarter, quarter), quarter), :] = total
+
+    def rs_copy(f, block, h):
+        if block == 0:
+            return copy(rs_out.at[f, 0, h], relay_in.at[f, h], rs_s, relay_r.at[f, h], dp=(up, down)[h])
+        return copy(rs_out.at[f, block, h], rs_in.at[f, block - 1, h], rs_s, rs_r.at[f, block - 1, h], dp=(up, down)[block - 1])
+
+    def dense_part(f, d, h):
+        return dense_f[f, pl.ds(pl.multiple_of(d * quarter + h * hq, hq), hq), :]
+
+    def sum_and_send(f):
         @pl.loop(0, n_dp)
-        def _(d):
-            add_to_dense(group, d, k == 0)
-
-    for k in range(len(head), len(batches)):
-        wait_inbox(k)
-
-    def rs_copies():
-        return (
-            copy(rs_out.at[0, 0], relay_in.at[0], rs_s, relay_r.at[0], dp=up),
-            copy(rs_out.at[0, 1], relay_in.at[1], rs_s, relay_r.at[1], dp=down),
-            copy(rs_out.at[1, 0], rs_in.at[0, 0], rs_s, rs_r.at[0, 0], dp=up),
-            copy(rs_out.at[1, 1], rs_in.at[0, 1], rs_s, rs_r.at[0, 1], dp=up),
-            copy(rs_out.at[2, 0], rs_in.at[1, 0], rs_s, rs_r.at[1, 0], dp=down),
-            copy(rs_out.at[2, 1], rs_in.at[1, 1], rs_s, rs_r.at[1, 1], dp=down),
-        )
-
-    def dense_part(d, h):
-        return dense_f[pl.ds(pl.multiple_of(d * quarter + h * hq, hq), hq), :]
-
-    far0, far1, up0, up1, down0, down1 = rs_copies()
-    tail_group = [src for group in tail for src in group]
-
-    @pl.loop(0, n_dp)
-    def _(k):
-        step_k = jnp.where(k == 0, 2, jnp.where(k == 1, 1, jnp.where(k == 2, 3, 0)))
-        add_to_dense(tail_group, lax.rem(y + step_k, n_dp), not head)
-
-        @pl.when(k == 0)
-        def _():
-            rs_out[0, 0] = dense_part(far, 0).astype(BF)
-            far0.start()
-            rs_out[0, 1] = dense_part(far, 1).astype(BF)
-            far1.start()
-
-        @pl.when(k == 1)
-        def _():
-            rs_out[1, 1] = dense_part(up, 1).astype(BF)
-            up1.start()
-
-        @pl.when(k == 2)
-        def _():
-            rs_out[2, 0] = dense_part(down, 0).astype(BF)
-            down0.start()
-
-    far0.wait_recv()
-    rs_out[1, 0] = (dense_part(up, 0) + relay_in[0].astype(F32)).astype(BF)
-    up0.start()
-    far1.wait_recv()
-    rs_out[2, 1] = (dense_part(down, 1) + relay_in[1].astype(F32)).astype(BF)
-    down1.start()
+        def _(k):
+            step_k = jnp.where(k == 0, 2, jnp.where(k == 1, 1, jnp.where(k == 2, 3, 0)))
+            quarter_sum(f, lax.rem(y + step_k, n_dp))
+
+            @pl.when(k == 0)
+            def _():
+                rs_out[f, 0, 0] = dense_part(f, far, 0).astype(BF)
+                rs_copy(f, 0, 0).start()
+                rs_out[f, 0, 1] = dense_part(f, far, 1).astype(BF)
+                rs_copy(f, 0, 1).start()
+
+            @pl.when(k == 1)
+            def _():
+                rs_out[f, 1, 1] = dense_part(f, up, 1).astype(BF)
+                rs_copy(f, 1, 1).start()
+
+            @pl.when(k == 2)
+            def _():
+                rs_out[f, 2, 0] = dense_part(f, down, 0).astype(BF)
+                rs_copy(f, 2, 0).start()
+
+    def relay(f):
+        rs_copy(f, 0, 0).wait_recv()
+        rs_out[f, 1, 0] = (dense_part(f, up, 0) + relay_in[f, 0].astype(F32)).astype(BF)
+        rs_copy(f, 1, 0).start()
+        rs_copy(f, 0, 1).wait_recv()
+        rs_out[f, 2, 1] = (dense_part(f, down, 1) + relay_in[f, 1].astype(F32)).astype(BF)
+        rs_copy(f, 2, 1).start()
+
+    wait_inbox(0)
+    sum_and_send(0)
+    relay(0)
+    wait_inbox(1)
+    sum_and_send(1)
+    relay(1)
 
     wait_others(in_x, nx, recv=hop_r.at[0])
     wait_others(in_z, nz, recv=hop_r.at[1])
@@ -542,20 +542,10 @@
     end_z[my_z] = mid_z[my_z]
     end_x[my_x] = mid_x[my_x]
 
-    ut[...] = jnp.zeros_like(ut)
-
-    @pl.loop(0, 2 * n_dp)
-    def _(piece):
-        block = negbuf[piece].reshape(chips * neg, width)
-        eb = et[piece].reshape(chips * neg, ex)
-        ut[...] += lax.dot_general(block, eb, (((0,), (0,)), ((), ())), preferred_element_type=F32)
-
-    g_q = INV_TEMP * (coef * pos_f[...] + jnp.transpose(ut[...]) * inv_tot)
-    grad_ref[...] = ((g_q - acc[...] * jnp.sum(acc[...] * g_q, axis=1, keepdims=True)) / q_norm).astype(BF)
-
     wait_all(req_out.at[pl.ds(0, n_item - 1)], send=req_s)
     wait_all(found.at[pl.ds(0, n_item - 1)], send=pos_s)
-    wait_all(outbox.at[pl.ds(0, n_item - 1)], send=g_s)
+    for f in range(2):
+        wait_all(outbox.at[f, pl.ds(0, n_item - 1)], send=g_s.at[f])
     wait_all(negbuf.at[mine, pl.ds(0, chips - 1)], send=neg_s)
     wait_all(nidbuf.at[mine, pl.ds(0, chips - 1)], send=nid_s)
     wait_all(negbuf.at[pl.ds(0, 3)], send=pc_s)
@@ -566,6 +556,20 @@
     wait_others(by_x, nx, send=hop_s.at[0])
     wait_others(by_z, nz, send=hop_s.at[1])
 
+    for f in range(2):
+        for block in (1, 2):
+            for h in range(2):
+                rs_copy(f, block, h).wait_recv()
+    for h in range(2):
+        both = [dense_part(f, y, h) + rs_in[f, 0, h].astype(F32) + rs_in[f, 1, h].astype(F32) for f in range(2)]
+        ag[y, h] = jnp.concatenate(both, axis=1).astype(BF)
+
+    def ag_copy(slot, h, dest):
+        return copy(ag.at[slot, h], ag.at[slot, h], ag_s, ag_r.at[slot, h], dp=dest)
+
+    ag_copy(y, 0, up).start()
+    ag_copy(y, 1, down).start()
+
     wait_others(end_z, nz, recv=hop_r.at[2])
     wait_others(end_x, nx, recv=hop_r.at[3])
     sums = jnp.concatenate([added(end_z), added(end_x)], axis=0)
@@ -581,23 +585,29 @@
 
     start_others(y, n_dp, part_copy)
 
+    ag_copy(y, 1, up).start()
+    ag_copy(y, 0, down).start()
+
     wait_others(y_in, n_dp, recv=y_r.at[0])
     y_sum[y] = added(y_in)
     start_others(y, n_dp, sum_copy)
-    up1.wait_recv()
-    up0.wait_recv()
-    down0.wait_recv()
-    down1.wait_recv()
-    for h in range(2):
-        ag[y, h] = (dense_part(y, h) + rs_in[0, h].astype(F32) + rs_in[1, h].astype(F32)).astype(BF)
-
-    def ag_copy(slot, h, dest):
-        return copy(ag.at[slot, h], ag.at[slot, h], ag_s, ag_r.at[slot, h], dp=dest)
-
-    ag_copy(y, 0, up).start()
-    ag_copy(y, 1, down).start()
-    ag_copy(y, 1, up).start()
-    ag_copy(y, 0, down).start()
+
+    wait_recv(ag.at[down, 0], ag_s, ag_r.at[down, 0], dp=down)
+    ag_copy(down, 0, up).start()
+    wait_recv(ag.at[up, 1], ag_s, ag_r.at[up, 1], dp=up)
+    ag_copy(up, 1, down).start()
+
+    ut[...] = jnp.zeros_like(ut)
+
+    @pl.loop(0, 2 * n_dp)
+    def _(piece):
+        block = negbuf[piece].reshape(chips * neg, width)
+        eb = et[piece].reshape(chips * neg, ex)
+        ut[...] += lax.dot_general(block, eb, (((0,), (0,)), ((), ())), preferred_element_type=F32)
+
+    g_q = INV_TEMP * (coef * pos_f[...] + jnp.transpose(ut[...]) * inv_tot)
+    grad_ref[...] = ((g_q - acc[...] * jnp.sum(acc[...] * g_q, axis=1, keepdims=True)) / q_norm).astype(BF)
+
     wait_others(y_sum, n_dp, recv=y_r.at[1])
     neg_sums = y_sum[...].reshape(n_dp * neg, width)
     neg_ids = jnp.concatenate([nidbuf[d * 2 + core, chip][:, :neg] for d in range(n_dp)], axis=1)
@@ -622,11 +632,6 @@
             step(d, h)
 
     step_both(y)
-
-    wait_recv(ag.at[down, 0], ag_s, ag_r.at[down, 0], dp=down)
-    ag_copy(down, 0, up).start()
-    wait_recv(ag.at[up, 1], ag_s, ag_r.at[up, 1], dp=up)
-    ag_copy(up, 1, down).start()
 
     wait_recv(ag.at[down, 1], ag_s, ag_r.at[down, 1], dp=down)
     wait_recv(ag.at[up, 0], ag_s, ag_r.at[up, 0], dp=up)
@@ -695,8 +700,8 @@
             pltpu.VMEM((2 * n_dp, chips, 1, LANES), F32),
             pltpu.VMEM((n_item, cap, width), BF),
             pltpu.VMEM((n_item, cap, width), BF),
-            pltpu.VMEM((n_item, cap, width), BF),
-            pltpu.VMEM((n_item, cap, width), BF),
+            pltpu.VMEM((2, n_item, cap, width // 2), BF),
+            pltpu.VMEM((2, n_item, cap, width // 2), BF),
             pltpu.VMEM((ex, width), F32),
             pltpu.VMEM((ex, width), F32),
             pltpu.VMEM((ex, width), BF),
@@ -716,10 +721,10 @@
             pltpu.VMEM((n_dp, neg, width), BF),
             pltpu.VMEM((n_dp, neg, width), BF),
             pltpu.VMEM((n_dp, neg, width), BF),
-            pltpu.VMEM((rows, width), F32),
-            pltpu.VMEM((3, 2, quarter // 2, width), BF),
-            pltpu.VMEM((2, quarter // 2, width), BF),
-            pltpu.VMEM((2, 2, quarter // 2, width), BF),
+            pltpu.VMEM((2, rows, width // 2), F32),
+            pltpu.VMEM((2, 3, 2, quarter // 2, width // 2), BF),
+            pltpu.VMEM((2, 2, quarter // 2, width // 2), BF),
+            pltpu.VMEM((2, 2, 2, quarter // 2, width // 2), BF),
             pltpu.VMEM((n_dp, 2, quarter // 2, width), BF),
             dma, dma,
             dma, dma,
@@ -729,11 +734,11 @@
             dma, dma((n_dp, 2)),
             dma, dma((n_dp, 2)),
             dma, dma((n_batches,)),
-            dma, dma((n_batches,)),
+            dma((2,)), dma((2, n_batches)),
             dma, dma,
             dma((4,)), dma((4,)),
             dma((2,)), dma((2,)),
-            dma, dma((2,)), dma((2, 2)),
+            dma, dma((2, 2)), dma((2, 2, 2)),
             dma, dma((n_dp, 2)),
             dma, dma,
         ],

time: 108 us -> 102 us (0.944)
  Pallas kernels: 107 us -> 101 us
    pallas_call x1, Pallas kernels: 104 us -> 98.9 us  [on_device(): pl.pallas_call(functools.partial(main_kernel, n_dp, n_item), out_shape=(p...]
where the time goes in v6:
time: 102 us
  Pallas kernels  101 us (99%)
    pallas_call x1, Pallas kernels, on_device(): pl.pallas_call(functools.partial(main_kernel, n_dp, n_item), out_shape=(p...  98.9 us
    pallas_call x1, Pallas kernels, on_device(): pl.pallas_call(write_kernel, out_shape=[jax.ShapeDtypeStruct(a.shape, a.d...  2.28 us

profile of v6, /device:TPU:1, one launch (start us, length us, event | category | flops | bytes accessed | tf_op | source)
XLA Modules:
  0.0 102.0 jit_solution(18162747207734000457)
XLA Ops:
  0.6 98.9 %training_step.1 = (bf16[1024,256]{1,0:T(8,128)(2,1)S(1)}, f32[1,1024]{1,0:T(1,128)S(1)}, f32[4096,256]{1,0:T(8,128)S(1)}, f32[1,4096]{1,0:T(1,128)S(1)}) custom-call(s32[48]{0:T(128)} %neg_s_ref.1, bf16[1024,256]{1,0:T(8,128)(2,1)} %q_hbm.1, f32[4096,256]{1,0:T(8,128)} %table_hbm.1, f32[1,4096]{1,0:T(1,128)} %bitcast.6, s32[1,1024]{1,0:T(1,128)} %bitcast.8, ...), custom_call_target="tpu_custom_call" | custom-call | flops 33822867456 | bytes 12582912 | tf_op jit(solution)/shard_map/training_step/pallas_call | solution.py:682
  99.6 2.3 %write_results.1 = (bf16[1024,256]{1,0:T(8,128)(2,1)}, f32[1,1024]{1,0:T(1,128)}, f32[4096,256]{1,0:T(8,128)}, f32[1,4096]{1,0:T(1,128)}) custom-call(bf16[1024,256]{1,0:T(8,128)(2,1)S(1)} %get-tuple-element.12.grad_v, f32[1,1024]{1,0:T(1,128)S(1)} %get-tuple-element.13.loss_v, f32[4096,256]{1,0:T(8,128)S(1)} %get-tuple-element.14.table_v, ...), custom_call_target="tpu_custom_call" | custom-call | tf_op jit(solution)/shard_map/write_results/pallas_call | solution.py:754

commit v7 on v6

--- a/solution.py
+++ b/solution.py
@@ -392,14 +392,6 @@
             def _():
                 g_copy(0, src, k).start()
 
-    @pl.loop(0, len(batches))
-    def _(k):
-        for src in one_of(k):
-
-            @pl.when(src != me)
-            def _():
-                g_copy(1, src, k).start()
-
     inbox[0, me] = outbox[0, me]
     inbox[1, me] = outbox[1, me]
 
@@ -419,6 +411,15 @@
     to_sib = copy(part.at[1 - core], sib_in, sib_s, sib_r, item=sibling)
     to_sib.start()
     pass2(core)
+
+    @pl.loop(0, len(batches))
+    def _(k):
+        for src in one_of(k):
+
+            @pl.when(src != me)
+            def _():
+                g_copy(1, src, k).start()
+
 
     to_sib.wait_recv()
 

time: 102 us -> 101 us (level)
  no operation moved by 1% of the time
where the time goes in v7:
time: 101 us
  Pallas kernels  100 us (99%)
    pallas_call x1, Pallas kernels, on_device(): pl.pallas_call(functools.partial(main_kernel, n_dp, n_item), out_shape=(p...  98.2 us
    pallas_call x1, Pallas kernels, on_device(): pl.pallas_call(write_kernel, out_shape=[jax.ShapeDtypeStruct(a.shape, a.d...  2.28 us

profile of v7, /device:TPU:1, one launch (start us, length us, event | category | flops | bytes accessed | tf_op | source)
XLA Modules:
  0.0 101.3 jit_solution(4124906684930634695)
XLA Ops:
  0.6 98.2 %training_step.1 = (bf16[1024,256]{1,0:T(8,128)(2,1)S(1)}, f32[1,1024]{1,0:T(1,128)S(1)}, f32[4096,256]{1,0:T(8,128)S(1)}, f32[1,4096]{1,0:T(1,128)S(1)}) custom-call(s32[48]{0:T(128)} %neg_s_ref.1, bf16[1024,256]{1,0:T(8,128)(2,1)} %q_hbm.1, f32[4096,256]{1,0:T(8,128)} %table_hbm.1, f32[1,4096]{1,0:T(1,128)} %bitcast.6, s32[1,1024]{1,0:T(1,128)} %bitcast.8, ...), custom_call_target="tpu_custom_call" | custom-call | flops 33822867456 | bytes 12582912 | tf_op jit(solution)/shard_map/training_step/pallas_call | solution.py:683
  98.8 2.3 %write_results.1 = (bf16[1024,256]{1,0:T(8,128)(2,1)}, f32[1,1024]{1,0:T(1,128)}, f32[4096,256]{1,0:T(8,128)}, f32[1,4096]{1,0:T(1,128)}) custom-call(bf16[1024,256]{1,0:T(8,128)(2,1)S(1)} %get-tuple-element.12.grad_v, f32[1,1024]{1,0:T(1,128)S(1)} %get-tuple-element.13.loss_v, f32[4096,256]{1,0:T(8,128)S(1)} %get-tuple-element.14.table_v, ...), custom_call_target="tpu_custom_call" | custom-call | tf_op jit(solution)/shard_map/write_results/pallas_call | solution.py:755
